TPU v7x, 256 devices: a whole 4x4x8 slice. The times are simulated.
256 devices in a mesh: island: 8 (over x, core), dap: 32 (over z, y).
Axes of the slice: x: 4, y: 4, z: 8, core: 2. Of those that a mesh axis runs over, the one named last changes fastest.
Arguments:
- pair: bfloat16 [8, 384, 384, 128], P('island', 'dap'), may hold values from -6 to 6
- cotangent: bfloat16 [8, 384, 384, 128], P('island', 'dap'), may hold values from -6 to 6
- res_count: int32 [8], P('island'), may hold values from 192 to 384, as said below
- w_left: bfloat16 [128, 128], replicated, may hold values from -0.5 to 0.5
- w_left_gate: bfloat16 [128, 128], replicated, may hold values from -0.5 to 0.5
- w_right: bfloat16 [128, 128], replicated, may hold values from -0.5 to 0.5
- w_right_gate: bfloat16 [128, 128], replicated, may hold values from -0.5 to 0.5
- w_gate: bfloat16 [128, 128], replicated, may hold values from -0.5 to 0.5
- w_out: bfloat16 [128, 128], replicated, may hold values from -0.5 to 0.5
Outputs:
- grad_pair: bfloat16 [8, 384, 384, 128], P('island', 'dap')
- grad_left: float32 [128, 128], replicated
- grad_left_gate: float32 [128, 128], replicated
- grad_right: float32 [128, 128], replicated
- grad_right_gate: float32 [128, 128], replicated
- grad_gate: float32 [128, 128], replicated
- grad_out: float32 [128, 128], replicated
Inputs may be any that keep to these rules, and one draw needn't show every extreme that they name: `res_count`: every count is at least 192, and some complex has all 384 residues.
All inputs are finite; a program needn't handle non-finite values.
Results may differ from a plain program's by a relative error of at most 0.0078.
Values may be sent and summed in bfloat16 or wider, within the bound.
No kernel may reach another device: no remote copies, remote signals or barrier semaphores. Data moves between devices by JAX's collectives and lax.ppermute only.
A program may use at most 128 MiB of HBM per device.

v0:
```python
import jax
import jax.numpy as jnp
from jax import lax
from jax.sharding import PartitionSpec as P


def on_device(
    pair, cotangent, res_count, w_left, w_left_gate, w_right, w_right_gate, w_gate, w_out
):
    cells = pair[0]
    count = res_count[0]
    rows_local = cells.shape[0]
    total = cells.shape[1]
    first_row = lax.axis_index("dap") * rows_local
    row_ids = first_row + jnp.arange(rows_local, dtype=jnp.int32)
    col_ids = jnp.arange(total, dtype=jnp.int32)
    pair_residue_mask = ((row_ids[:, None] < count) & (col_ids[None, :] < count)).astype(
        jnp.float32
    )
    lproj = jnp.einsum("ikd,dc->cik", cells, w_left, preferred_element_type=jnp.float32)
    lgate = jax.nn.sigmoid(
        jnp.einsum("ikd,dc->cik", cells, w_left_gate, preferred_element_type=jnp.float32)
    )
    right_projected = jnp.einsum("ikd,dc->cik", cells, w_right, preferred_element_type=jnp.float32)
    right_gate_value = jax.nn.sigmoid(
        jnp.einsum("ikd,dc->cik", cells, w_right_gate, preferred_element_type=jnp.float32)
    )
    left_rows = (pair_residue_mask * lgate * lproj).astype(jnp.bfloat16)
    right_rows = (pair_residue_mask * right_gate_value * right_projected).astype(jnp.bfloat16)
    left_chan, right_chan = (
        lax.all_to_all(left_rows, "dap", split_axis=0, concat_axis=1, tiled=True),
        lax.all_to_all(right_rows, "dap", split_axis=0, concat_axis=1, tiled=True),
    )
    edge_chan = jnp.einsum(
        "cik,cjk->cij", left_chan, right_chan, preferred_element_type=jnp.float32
    ).astype(jnp.bfloat16)
    edge_rows = lax.all_to_all(edge_chan, "dap", split_axis=1, concat_axis=0, tiled=True)
    edge_f = edge_rows.astype(jnp.float32)
    mean_shifted = edge_f - jnp.mean(edge_f, axis=0)
    inverse_deviation = lax.rsqrt(jnp.mean(mean_shifted * mean_shifted, axis=0) + 1e-05)
    standardized_input = mean_shifted * inverse_deviation
    layer_normed = (standardized_input * pair_residue_mask).astype(jnp.bfloat16)
    gate_sig = jax.nn.sigmoid(
        jnp.einsum("ijd,do->ijo", cells, w_gate, preferred_element_type=jnp.float32)
    )
    linear_out = jnp.einsum("cij,co->ijo", layer_normed, w_out, preferred_element_type=jnp.float32)
    grad_in = cotangent[0].astype(jnp.float32)
    dscaled = (grad_in * gate_sig).astype(jnp.bfloat16)
    dgate_pre = (grad_in * linear_out * gate_sig * (1.0 - gate_sig)).astype(jnp.bfloat16)
    normed_gradient = jnp.einsum("ijo,co->cij", dscaled, w_out, preferred_element_type=jnp.float32)
    dedge_rows = (
        pair_residue_mask
        * inverse_deviation
        * (
            normed_gradient
            - jnp.mean(normed_gradient, axis=0)
            - standardized_input * jnp.mean(normed_gradient * standardized_input, axis=0)
        )
    ).astype(jnp.bfloat16)
    dedge_chan = lax.all_to_all(dedge_rows, "dap", split_axis=0, concat_axis=1, tiled=True)
    dleft_chan = jnp.einsum(
        "cij,cjk->cik", dedge_chan, right_chan, preferred_element_type=jnp.float32
    ).astype(jnp.bfloat16)
    dright_chan = jnp.einsum(
        "cij,cik->cjk", dedge_chan, left_chan, preferred_element_type=jnp.float32
    ).astype(jnp.bfloat16)
    dleft_rows, right_row_gradient = (
        lax.all_to_all(dleft_chan, "dap", split_axis=1, concat_axis=0, tiled=True),
        lax.all_to_all(dright_chan, "dap", split_axis=1, concat_axis=0, tiled=True),
    )
    dlf = dleft_rows.astype(jnp.float32) * pair_residue_mask
    right_full_gradient = right_row_gradient.astype(jnp.float32) * pair_residue_mask
    dlin_left = (dlf * lgate).astype(jnp.bfloat16)
    dgl = (dlf * lproj * lgate * (1.0 - lgate)).astype(jnp.bfloat16)
    right_linear_gradient = (right_full_gradient * right_gate_value).astype(jnp.bfloat16)
    right_gate_gradient = (
        right_full_gradient * right_projected * right_gate_value * (1.0 - right_gate_value)
    ).astype(jnp.bfloat16)
    grad_cells = (
        jnp.einsum("ijo,do->ijd", dgate_pre, w_gate, preferred_element_type=jnp.float32)
        + jnp.einsum("cij,dc->ijd", dlin_left, w_left, preferred_element_type=jnp.float32)
        + jnp.einsum("cij,dc->ijd", dgl, w_left_gate, preferred_element_type=jnp.float32)
        + jnp.einsum(
            "cij,dc->ijd", right_linear_gradient, w_right, preferred_element_type=jnp.float32
        )
        + jnp.einsum(
            "cij,dc->ijd", right_gate_gradient, w_right_gate, preferred_element_type=jnp.float32
        )
    ).astype(jnp.bfloat16)
    part_left = jnp.einsum("ikd,cik->dc", cells, dlin_left, preferred_element_type=jnp.float32)
    part_lgate = jnp.einsum("ikd,cik->dc", cells, dgl, preferred_element_type=jnp.float32)
    part_right = jnp.einsum(
        "ikd,cik->dc", cells, right_linear_gradient, preferred_element_type=jnp.float32
    )
    part_rgate = jnp.einsum(
        "ikd,cik->dc", cells, right_gate_gradient, preferred_element_type=jnp.float32
    )
    part_gate = jnp.einsum("ijd,ijo->do", cells, dgate_pre, preferred_element_type=jnp.float32)
    part_out = jnp.einsum("cij,ijo->co", layer_normed, dscaled, preferred_element_type=jnp.float32)
    totals = lax.psum(
        (part_left, part_lgate, part_right, part_rgate, part_gate, part_out), ("island", "dap")
    )
    return (grad_cells[None], totals[0], totals[1], totals[2], totals[3], totals[4], totals[5])


def solution(mesh):
    in_specs = (
        P("island", "dap", None, None),
        P("island", "dap", None, None),
        P("island"),
        P(),
        P(),
        P(),
        P(),
        P(),
        P(),
    )
    out_specs = (P("island", "dap", None, None), P(), P(), P(), P(), P(), P())
    return jax.shard_map(
        on_device, mesh=mesh, in_specs=in_specs, out_specs=out_specs, check_vma=False
    )
```

profile of v0, /device:TPU:1, one launch (start us, length us, event | category | flops | bytes accessed | tf_op | source)
XLA Modules:
  0.0 578.6 jit_solution(16173596736252737961)
XLA Ops:
  8.5 3.0 add_divide_fusion.2
  12.2 2.3 add_divide_fusion.1
  14.6 4.7 multiply_convert_fusion.6
  21.3 12.0 %all-to-all-start = ((bf16[128,12,384]{2,1,0:T(8,128)(2,1)}), bf16[128,12,384]{2,1,0:T(8,128)(2,1)S(1)}, u32[]{:S(2)}, u32[]{:S(2)}) async-start(bf16[128,12,384]{2,1,0:T(8,128)(2,1)} %copy.70), calls=%async_computation | async-start | bytes 3145728 | tf_op jit(solution)/shard_map/all_to_all | solution.py:31
  33.3 3.1 copy.74
  36.5 34.7 %all-to-all-done = bf16[128,12,384]{2,1,0:T(8,128)(2,1)S(1)} async-done(((bf16[128,12,384]{2,1,0:T(8,128)(2,1)}), bf16[128,12,384]{2,1,0:T(8,128)(2,1)S(1)}, u32[]{:S(2)}, u32[]{:S(2)}) %all-to-all-start) | async-done | bytes 1179680 | tf_op jit(solution)/shard_map/all_to_all | solution.py:31
  71.2 5.9 %all-to-all-start.1 = ((bf16[128,12,384]{2,1,0:T(8,128)(2,1)}), bf16[128,12,384]{2,1,0:T(8,128)(2,1)}, u32[]{:S(2)}, u32[]{:S(2)}) async-start(bf16[128,12,384]{2,1,0:T(8,128)(2,1)} %copy.74), calls=%async_computation.1 | async-start | bytes 3145728 | tf_op jit(solution)/shard_map/all_to_all | solution.py:32
  78.6 34.3 %all-to-all-done.1 = bf16[128,12,384]{2,1,0:T(8,128)(2,1)} async-done(((bf16[128,12,384]{2,1,0:T(8,128)(2,1)}), bf16[128,12,384]{2,1,0:T(8,128)(2,1)}, u32[]{:S(2)}, u32[]{:S(2)}) %all-to-all-start.1) | async-done | bytes 1179680 | tf_op jit(solution)/shard_map/all_to_all | solution.py:32
  116.7 1.9 copy.78
  118.7 7.5 %all-to-all-start.2 = ((bf16[4,384,384]{2,0,1:T(4,128)(2,1)}), bf16[4,384,384]{2,0,1:T(4,128)(2,1)S(1)}, u32[]{:S(2)}, u32[]{:S(2)}) async-start(bf16[4,384,384]{2,0,1:T(4,128)(2,1)} %copy.78), calls=%async_computation.2 | async-start | bytes 2359296 | tf_op jit(solution)/shard_map/all_to_all | solution.py:37
  126.1 2.2 add_divide_fusion
  128.4 25.0 %all-to-all-done.2 = bf16[4,384,384]{2,0,1:T(4,128)(2,1)S(1)} async-done(((bf16[4,384,384]{2,0,1:T(4,128)(2,1)}), bf16[4,384,384]{2,0,1:T(4,128)(2,1)S(1)}, u32[]{:S(2)}, u32[]{:S(2)}) %all-to-all-start.2) | async-done | bytes 1179680 | tf_op jit(solution)/shard_map/all_to_all | solution.py:37
  155.7 1.9 copy.79
  157.6 2.7 reshape.113
  160.3 2.8 bitcast_reduce_fusion
  164.7 43.3 %all_to_all.81 = bf16[128,12,384]{2,1,0:T(8,128)(2,1)S(1)} all-to-all(bf16[128,12,384]{2,1,0:T(8,128)(2,1)S(1)} %copy.81), channel_id=1, replica_groups=mesh['island'=8,'dap'=32] {'dap'}, dimensions={0} | all-to-all | bytes 2359296 | tf_op jit(solution)/shard_map/all_to_all | solution.py:60
  209.5 3.4 copy.89
  212.8 2.5 convolution_convert_fusion
  215.4 1.9 copy.91
  217.3 7.0 %all-to-all-start.5 = ((bf16[4,384,384]{2,0,1:T(4,128)(2,1)}), bf16[4,384,384]{2,0,1:T(4,128)(2,1)}, u32[]{:S(2)}, u32[]{:S(2)}) async-start(bf16[4,384,384]{2,0,1:T(4,128)(2,1)} %copy.91), calls=%async_computation.5 | async-start | bytes 2359296 | tf_op jit(solution)/shard_map/all_to_all | solution.py:69
  224.3 2.6 convolution_convert_fusion.1
  228.8 22.2 %all-to-all-done.5 = bf16[4,384,384]{2,0,1:T(4,128)(2,1)} async-done(((bf16[4,384,384]{2,0,1:T(4,128)(2,1)}), bf16[4,384,384]{2,0,1:T(4,128)(2,1)}, u32[]{:S(2)}, u32[]{:S(2)}) %all-to-all-start.5) | async-done | bytes 1179680 | tf_op jit(solution)/shard_map/all_to_all | solution.py:69
  251.0 8.1 %all-to-all-start.4 = ((bf16[4,384,384]{2,0,1:T(4,128)(2,1)}), bf16[4,384,384]{2,0,1:T(4,128)(2,1)}, u32[]{:S(2)}, u32[]{:S(2)}) async-start(bf16[4,384,384]{2,0,1:T(4,128)(2,1)} %copy.85), calls=%async_computation.4 | async-start | bytes 2359296 | tf_op jit(solution)/shard_map/all_to_all | solution.py:68
  259.4 2.9 fusion.2
  271.7 14.2 %all-to-all-done.4 = bf16[4,384,384]{2,0,1:T(4,128)(2,1)} async-done(((bf16[4,384,384]{2,0,1:T(4,128)(2,1)}), bf16[4,384,384]{2,0,1:T(4,128)(2,1)}, u32[]{:S(2)}, u32[]{:S(2)}) %all-to-all-start.4) | async-done | bytes 1179680 | tf_op jit(solution)/shard_map/all_to_all | solution.py:68
  287.4 2.0 copy.86
  289.4 3.8 reshape.114
  293.2 5.8 %multiply_convert_fusion.3 = (bf16[128,12,384]{2,0,1:T(8,128)(2,1)S(1)}, bf16[128,12,384]{2,0,1:T(8,128)(2,1)S(1)}, bf16[128,12,384]{2,0,1:T(8,128)(2,1)S(1)}, bf16[128,12,384]{2,0,1:T(8,128)(2,1)S(1)}) fusion(f32[128,12,384]{2,0,1:T(8,128)} %add_divide_fusion.2, f32[128,12,384]{2,0,1:T(8,128)} %reshape.114, f32[12,384]{1,0:T(8,128)} %copy-done.12, ...), kind=kLoop, calls=%fused_computation.20 | loop fusion | flops 9437184 | bytes 18892800 | tf_op jit(solution)/shard_map/convert_element_type | solution.py:73
  303.2 2.0 fusion.60
  306.3 1.9 fusion.57
  309.4 5.2 fusion.8
  314.6 247.9 %all-reduce.3.cloned.1.call-done = (f32[128,128]{0,1:T(8,128)}, f32[128,128]{0,1:T(8,128)}, f32[128,128]{0,1:T(8,128)}, f32[128,128]{0,1:T(8,128)}, f32[128,128]{0,1:T(8,128)}, /*index=5*/f32[128,128]{1,0:T(8,128)}) async-done(((f32[128,128]{0,1:T(8,128)}, f32[128,128]{0,1:T(8,128)}, f32[128,128]{0,1:T(8,128)}, f32[128,128]{0,1:T(8,128)}, f32[128,128]{0,1:T(8,128)}, /*index=5*/f32[128,128]{1,0:T(8,128)}), ...) | async-done | bytes 393232 | tf_op jit(solution)/shard_map/psum | solution.py:100
  (86 shorter events, 42.8 us)
Async XLA Ops:
  7.2 1.3 copy-start
  8.5 3.0 copy-start.16
  11.5 0.8 copy-start.23
  12.2 2.4 copy-start.1
  14.6 4.7 copy-start.12
  21.3 49.9 %all-to-all-start = ((bf16[128,12,384]{2,1,0:T(8,128)(2,1)}), bf16[128,12,384]{2,1,0:T(8,128)(2,1)S(1)}, u32[]{:S(2)}, u32[]{:S(2)}) async-start(bf16[128,12,384]{2,1,0:T(8,128)(2,1)} %copy.70), calls=%async_computation | async-start | bytes 3145728 | tf_op jit(solution)/shard_map/all_to_all | solution.py:31
  71.2 41.7 %all-to-all-start.1 = ((bf16[128,12,384]{2,1,0:T(8,128)(2,1)}), bf16[128,12,384]{2,1,0:T(8,128)(2,1)}, u32[]{:S(2)}, u32[]{:S(2)}) async-start(bf16[128,12,384]{2,1,0:T(8,128)(2,1)} %copy.74), calls=%async_computation.1 | async-start | bytes 3145728 | tf_op jit(solution)/shard_map/all_to_all | solution.py:32
  78.6 37.2 %copy-start.8 = (bf16[32,4,12,384]{3,1,2,0:T(4,128)(2,1)S(1)}, bf16[32,4,12,384]{3,1,2,0:T(4,128)(2,1)}, u32[]{:S(2)}) copy-start(bf16[32,4,12,384]{3,1,2,0:T(4,128)(2,1)} %copy.71) | copy-start | bytes 3538948
  114.7 1.0 copy-start.7
  116.7 9.4 %copy-start.20 = (bf16[128,128]{1,0:T(8,128)(2,1)S(1)}, bf16[128,128]{1,0:T(8,128)(2,1)}, u32[]{:S(2)}) copy-start(bf16[128,128]{1,0:T(8,128)(2,1)} %param.16) | copy-start | bytes 98308
  118.7 34.7 %all-to-all-start.2 = ((bf16[4,384,384]{2,0,1:T(4,128)(2,1)}), bf16[4,384,384]{2,0,1:T(4,128)(2,1)S(1)}, u32[]{:S(2)}, u32[]{:S(2)}) async-start(bf16[4,384,384]{2,0,1:T(4,128)(2,1)} %copy.78), calls=%async_computation.2 | async-start | bytes 2359296 | tf_op jit(solution)/shard_map/all_to_all | solution.py:37
  154.2 0.8 copy-start.9
  160.3 2.9 copy-start.10
  160.3 2.9 copy-start.14
  160.3 2.9 copy-start.19
  217.3 33.7 %all-to-all-start.5 = ((bf16[4,384,384]{2,0,1:T(4,128)(2,1)}), bf16[4,384,384]{2,0,1:T(4,128)(2,1)}, u32[]{:S(2)}, u32[]{:S(2)}) async-start(bf16[4,384,384]{2,0,1:T(4,128)(2,1)} %copy.91), calls=%async_computation.5 | async-start | bytes 2359296 | tf_op jit(solution)/shard_map/all_to_all | solution.py:69
  251.0 34.8 %all-to-all-start.4 = ((bf16[4,384,384]{2,0,1:T(4,128)(2,1)}), bf16[4,384,384]{2,0,1:T(4,128)(2,1)}, u32[]{:S(2)}, u32[]{:S(2)}) async-start(bf16[4,384,384]{2,0,1:T(4,128)(2,1)} %copy.85), calls=%async_computation.4 | async-start | bytes 2359296 | tf_op jit(solution)/shard_map/all_to_all | solution.py:68
  259.1 303.3 %all-reduce.3.cloned.1.call-start = ((), (), s32[]{:S(2)}) async-start(), calls=%async_computation.6 | async-start | bytes 786432 | tf_op jit(solution)/shard_map/psum | solution.py:100
  262.3 1.2 copy-start.21
  262.3 3.1 copy-start.13
  262.3 3.1 copy-start.15
  263.5 2.2 copy-start.3
  263.5 2.8 copy-start.5
  263.5 2.8 copy-start.11
  289.4 3.8 copy-start.2
  299.0 9.2 %copy-start.4 = (bf16[128,12,384]{2,0,1:T(8,128)(2,1)}, bf16[128,12,384]{2,0,1:T(8,128)(2,1)S(1)}, u32[]{:S(2)}) copy-start(bf16[128,12,384]{2,0,1:T(8,128)(2,1)S(1)} %get-tuple-element.40) | copy-start | bytes 3538948
  299.0 1.1 copy-start.17
  300.2 3.1 copy-start.22
  303.2 3.1 copy-start.18
  306.3 3.1 copy-start.6
Sparse Core Ops, SparseCore 0:
  309.5 252.8 all-reduce.2
where the time goes:
time: 580 us; the launch traced here: 579 us
  waiting for transfers between devices  378 us (65%)
  local copies, waits for them, and re-layouts  44.7 us (8%)
  matrix products  44.3 us (8%)
  blocking collectives  43.3 us (7%)
  starting transfers between devices  40.8 us (7%)
  between operations  15.1 us (3%)
  other arithmetic  12.1 us (2%)
    psum x1, waiting for transfers between devices, on_device(): lax.psum((part_left, part_lgate, part_right, part_rgate, part_gate, part_...  248 us
    all_to_all x1, blocking collectives, on_device(): lax.all_to_all(dedge_rows, 'dap', split_axis=0, concat_axis=1, tiled=True)  43.3 us
    all_to_all x1, waiting for transfers between devices, on_device(): lax.all_to_all(left_rows, 'dap', split_axis=0, concat_axis=1, tiled=True)  34.7 us
    all_to_all x1, waiting for transfers between devices, on_device(): lax.all_to_all(right_rows, 'dap', split_axis=0, concat_axis=1, tiled=True)  34.3 us
    all_to_all x1, waiting for transfers between devices, on_device(): lax.all_to_all(edge_chan, 'dap', split_axis=1, concat_axis=0, tiled=True)  25 us
    all_to_all x1, waiting for transfers between devices, on_device(): lax.all_to_all(dright_chan, 'dap', split_axis=1, concat_axis=0, tiled=True)  22.2 us
    all_to_all x1, waiting for transfers between devices, on_device(): lax.all_to_all(dleft_chan, 'dap', split_axis=1, concat_axis=0, tiled=True)  14.2 us
    unnamed x54, local copies, waits for them, and re-layouts  12.2 us
  transfers between devices with their start and end apart: 6, of which 6 were waited for; matrix products, arithmetic and copies ran while one was open for 5% of the time, Pallas kernels for 0%

commit v1 on v0

v1 whole, which is shorter than its diff:
```python
import jax
import jax.numpy as jnp
from jax import lax
from jax.experimental import pallas as pl
from jax.experimental.pallas import tpu as pltpu
from jax.sharding import PartitionSpec as P

F32 = jnp.float32
BF16 = jnp.bfloat16
C = 128
HI = lax.Precision.HIGHEST


def dot(a, b, ca, cb, precision=None):
    return lax.dot_general(
        a, b, (((ca,), (cb,)), ((), ())), preferred_element_type=F32, precision=precision
    )


def iota(shape, dim):
    return lax.broadcasted_iota(jnp.int32, shape, dim)


def pick(side):
    row, chan = iota((2 * C, C), 0), iota((2 * C, C), 1)
    hit = ((row % 8) // 4 == side) & (chan == (row // 8) * 4 + row % 4)
    return hit.astype(F32)


def spread_rows(w_out):
    parts = [dot(pick(side).astype(BF16), w_out, 1, 0) for side in range(2)]
    return jnp.concatenate(parts, axis=1).astype(BF16)


def both_projections(w_left, w_left_gate, w_right, w_right_gate):
    on_left, on_right = pick(0).astype(BF16), pick(1).astype(BF16)
    proj = dot(on_left, w_left, 1, 1) + dot(on_right, w_right, 1, 1)
    gate = dot(on_left, w_left_gate, 1, 1) + dot(on_right, w_right_gate, 1, 1)
    return jnp.concatenate([proj, gate], axis=0).astype(BF16)


def row_mask(count, row, shape):
    return jnp.where((row < count) & (iota(shape, len(shape) - 1) < count), 1.0, 0.0)


def first_row(rows):
    return lax.axis_index("dap") * rows


def project_kernel(count_ref, z_ref, wl_ref, wlg_ref, wr_ref, wrg_ref, out_ref, w_ref):
    rows, total, _ = z_ref.shape
    count = count_ref[0]
    start = first_row(rows)
    w_ref[...] = both_projections(wl_ref[...], wlg_ref[...], wr_ref[...], wrg_ref[...])

    def body(m, carry):
        halves = []
        for h in range(2):
            i = 2 * m + h
            pg = dot(w_ref[...], z_ref[i], 1, 1)
            mask = row_mask(count, start + i, (1, total))
            made = mask * jax.nn.sigmoid(pg[2 * C :]) * pg[: 2 * C]
            halves.append(made.reshape(32, 8, total))
        at = pl.multiple_of(16 * m, 16)
        out_ref[:, pl.ds(at, 16), :] = jnp.concatenate(halves, axis=1).astype(BF16)
        return carry

    lax.fori_loop(0, rows // 2, body, 0)


def put_wide(ref, at, rows, value):
    for n in range(ref.shape[0]):
        ref[n, pl.ds(at, rows), :] = value[:, n * C : (n + 1) * C]


def take(ref, first, count, step):
    return jnp.concatenate(
        [ref[n, pl.ds(first, count, stride=step), :] for n in range(ref.shape[0])], axis=1
    )


def put(ref, first, count, step, value):
    for n in range(ref.shape[0]):
        ref[n, pl.ds(first, count, stride=step), :] = value[:, n * C : (n + 1) * C]


def get_rows(ref, at, rows):
    return jnp.concatenate([ref[n, pl.ds(at, rows), :] for n in range(ref.shape[0])], axis=1)


def edges_kernel(x_ref, out_ref, lr_ref, wide_ref, prod_ref):
    devices, block, total = x_ref.shape

    def widen(s, carry):
        put_wide(wide_ref, pl.multiple_of(s * block, block), block, x_ref[s].astype(F32))
        return carry

    lax.fori_loop(0, devices, widen, 0)
    for c in range(4):
        left = take(wide_ref, c, total, 8).astype(BF16)
        right = take(wide_ref, 4 + c, total, 8).astype(BF16)
        lr_ref[c] = left
        lr_ref[4 + c] = right
        put(prod_ref, c, total, 4, dot(left, right, 1, 1))

    def narrow(s, carry):
        at = pl.multiple_of(s * (block // 2), block // 2)
        out_ref[s] = get_rows(prod_ref, at, block // 2).astype(BF16)
        return carry

    lax.fori_loop(0, devices, narrow, 0)


def gates_kernel(z_ref, g_ref, wg_ref, wo_ref, ds_ref, fac_ref, dn_ref, wgt_ref, wx_ref):
    rows = z_ref.shape[0]
    wgt_ref[...] = wg_ref[...].astype(F32).T.astype(BF16)
    wx_ref[...] = spread_rows(wo_ref[...])

    def body(m, carry):
        for h in range(2):
            i = 2 * m + h
            gate = jax.nn.sigmoid(dot(wgt_ref[...], z_ref[i], 1, 1))
            scaled = g_ref[i].astype(F32).T * gate
            ds_ref[m, h * C : (h + 1) * C, :] = scaled.astype(BF16)
            fac_ref[m, h * C : (h + 1) * C, :] = scaled * (1.0 - gate)
        dn_ref[m] = dot(wx_ref[...], ds_ref[m], 1, 0)
        return carry

    lax.fori_loop(0, rows // 2, body, 0)


def chan_mean(x):
    s = jnp.sum(x, axis=0)
    top = iota(s.shape, 0) < 4
    first = jnp.sum(jnp.where(top, s, 0.0), axis=0, keepdims=True)
    second = jnp.sum(jnp.where(top, 0.0, s), axis=0, keepdims=True)
    return jnp.where(top, first, second) * (1.0 / C)


def norm_kernel(count_ref, e_ref, dn_ref, de_ref, nm_ref):
    devices, block, total = e_ref.shape
    rows = block // 4
    count = count_ref[0]
    start = first_row(rows)

    def body(q, carry):
        at = pl.multiple_of(16 * q, 16)
        e_all = e_ref[:, pl.ds(at, 16), :].astype(F32)
        halves = []
        for h in range(2):
            e = e_all[:, 8 * h : 8 * h + 8, :]
            row = start + 4 * q + 2 * h + iota((8, total), 0) // 4
            mask = row_mask(count, row, (8, total))
            shifted = e - chan_mean(e)[None]
            rs = lax.rsqrt(chan_mean(shifted * shifted) + 1e-05)
            xhat = shifted * rs[None]
            nm_ref[2 * q + h] = (xhat * mask[None]).reshape(2 * C, total).astype(BF16)
            dn = dn_ref[2 * q + h].reshape(32, 8, total)
            m1 = chan_mean(dn)
            m2 = chan_mean(dn * xhat)
            halves.append((mask * rs)[None] * (dn - m1[None] - xhat * m2[None]))
        de_ref[:, pl.ds(at, 16), :] = jnp.concatenate(halves, axis=1).astype(BF16)
        return carry

    lax.fori_loop(0, rows // 4, body, 0)


def linear_kernel(z_ref, nm_ref, ds_ref, fac_ref, wo_ref, dg_ref, gg_ref, go_ref, wx_ref, ga_ref, oa_ref):
    rows = z_ref.shape[0]
    wx_ref[...] = spread_rows(wo_ref[...]).astype(F32).T.astype(BF16)
    ga_ref[...] = jnp.zeros_like(ga_ref)
    oa_ref[...] = jnp.zeros_like(oa_ref)

    def body(m, carry):
        lin = dot(wx_ref[...], nm_ref[m], 1, 0)
        dg_ref[m] = (lin * fac_ref[m]).astype(BF16)
        for h in range(2):
            ga_ref[...] += dot(dg_ref[m, h * C : (h + 1) * C, :], z_ref[2 * m + h], 1, 0)
        oa_ref[...] += dot(nm_ref[m], ds_ref[m], 1, 1)
        return carry

    lax.fori_loop(0, rows // 2, body, 0)
    gg_ref[...] = ga_ref[...].T
    go_ref[...] = dot(pick(0), oa_ref[:, :C], 0, 0, HI) + dot(pick(1), oa_ref[:, C:], 0, 0, HI)


def back_kernel(x_ref, lr_ref, out_ref, wide_ref, prod_ref):
    devices, block, total = x_ref.shape

    def widen(s, carry):
        put_wide(wide_ref, pl.multiple_of(s * block, block), block, x_ref[s].astype(F32))
        return carry

    lax.fori_loop(0, devices, widen, 0)
    for c in range(4):
        de = take(wide_ref, c, total, 4)
        put(prod_ref, c, total, 8, dot(de.astype(BF16), lr_ref[4 + c], 1, 0))
        put(prod_ref, 4 + c, total, 8, dot(de.T.astype(BF16), lr_ref[c], 1, 0))

    def narrow(s, carry):
        at = pl.multiple_of(s * (2 * block), 2 * block)
        out_ref[s] = get_rows(prod_ref, at, 2 * block).astype(BF16)
        return carry

    lax.fori_loop(0, devices, narrow, 0)


def weights_kernel(
    count_ref, z_ref, d_ref, wl_ref, wlg_ref, wr_ref, wrg_ref, gg_ref, go_ref, x_ref, out_ref, w_ref, acc_ref
):
    rows, total, _ = z_ref.shape
    count = count_ref[0]
    start = first_row(rows)
    w_ref[...] = both_projections(wl_ref[...], wlg_ref[...], wr_ref[...], wrg_ref[...])
    acc_ref[...] = jnp.zeros_like(acc_ref)

    def body(m, carry):
        at = pl.multiple_of(16 * m, 16)
        both = d_ref[:, pl.ds(at, 16), :].astype(F32)
        for h in range(2):
            i = 2 * m + h
            d = both[:, 8 * h : 8 * h + 8, :].reshape(2 * C, total)
            d = d * row_mask(count, start + i, (1, total))
            pg = dot(w_ref[...], z_ref[i], 1, 1)
            gate = jax.nn.sigmoid(pg[2 * C :])
            dlin = d * gate
            x_ref[i, : 2 * C, :] = dlin.astype(BF16)
            x_ref[i, 2 * C :, :] = (dlin * pg[: 2 * C] * (1.0 - gate)).astype(BF16)
            acc_ref[...] += dot(x_ref[i], z_ref[i], 1, 0)
        return carry

    lax.fori_loop(0, rows // 2, body, 0)
    on_left, on_right = pick(0), pick(1)
    out_ref[0 * C : 1 * C, :] = dot(acc_ref[: 2 * C, :], on_left, 0, 0, HI)
    out_ref[1 * C : 2 * C, :] = dot(acc_ref[2 * C :, :], on_left, 0, 0, HI)
    out_ref[2 * C : 3 * C, :] = dot(acc_ref[: 2 * C, :], on_right, 0, 0, HI)
    out_ref[3 * C : 4 * C, :] = dot(acc_ref[2 * C :, :], on_right, 0, 0, HI)
    out_ref[4 * C : 5 * C, :] = gg_ref[...]
    out_ref[5 * C : 6 * C, :] = go_ref[...]


def pair_kernel(x_ref, dg_ref, wl_ref, wlg_ref, wr_ref, wrg_ref, wg_ref, out_ref, w_ref):
    rows = x_ref.shape[0]
    w_ref[...] = both_projections(wl_ref[...], wlg_ref[...], wr_ref[...], wrg_ref[...]).astype(F32).T.astype(BF16)

    def body(m, carry):
        for h in range(2):
            i = 2 * m + h
            made = dot(w_ref[...], x_ref[i], 1, 0) + dot(wg_ref[...], dg_ref[m, h * C : (h + 1) * C, :], 1, 0)
            out_ref[0, i] = made.T.astype(BF16)
        return carry

    lax.fori_loop(0, rows // 2, body, 0)


def call(body, outs, scratch, flops, *args, smem=()):
    specs = [
        pl.BlockSpec(memory_space=pltpu.SMEM if n in smem else pltpu.VMEM) for n in range(len(args))
    ]
    shapes = [jax.ShapeDtypeStruct(s, t) for s, t in outs]
    out_specs = [pl.BlockSpec(memory_space=pltpu.VMEM)] * len(outs)
    if len(outs) == 1:
        shapes, out_specs = shapes[0], out_specs[0]
    moved = sum(a.size * a.dtype.itemsize for a in args)
    return pl.pallas_call(
        body,
        out_shape=shapes,
        in_specs=specs,
        out_specs=out_specs,
        scratch_shapes=[pltpu.VMEM(s, t) for s, t in scratch],
        compiler_params=pltpu.CompilerParams(vmem_limit_bytes=40 << 20),
        cost_estimate=pl.CostEstimate(flops=flops, bytes_accessed=moved, transcendentals=0),
    )(*args)


def exchange(x, axis):
    return lax.all_to_all(x, axis, split_axis=0, concat_axis=0, tiled=True)


def on_device(
    pair, cotangent, res_count, w_left, w_left_gate, w_right, w_right_gate, w_gate, w_out
):
    z, g = pair[0], cotangent[0]
    rows, total, _ = z.shape
    pairs = rows // 2
    sides = (w_left, w_left_gate, w_right, w_right_gate)
    mega = 10**6

    blocks = call(
        project_kernel, [((32, 8 * rows, total), BF16)], [((4 * C, C), BF16)], 4000 * mega,
        res_count, z, *sides, smem=(0,),
    )
    blocks = exchange(blocks, "dap")
    scaled, factor, dnormed = call(
        gates_kernel,
        [((pairs, 2 * C, total), BF16), ((pairs, 2 * C, total), F32), ((pairs, 2 * C, total), F32)],
        [((C, C), BF16), ((2 * C, 2 * C), BF16)], 4000 * mega,
        z, g, w_gate, w_out,
    )
    edges, lr = call(
        edges_kernel,
        [((32, 4 * rows, total), BF16), ((8, total, total), BF16)],
        [((total // C, 8 * total, C), F32), ((total // C, 4 * total, C), F32)], 4000 * mega,
        blocks,
    )
    edges = exchange(edges, "dap")
    dedges, normed = call(
        norm_kernel,
        [((32, 4 * rows, total), BF16), ((pairs, 2 * C, total), BF16)], [], 4000 * mega,
        res_count, edges, dnormed, smem=(0,),
    )
    dedges = exchange(dedges, "dap")
    dgate, part_gate, part_out = call(
        linear_kernel,
        [((pairs, 2 * C, total), BF16), ((C, C), F32), ((C, C), F32)],
        [((2 * C, 2 * C), BF16), ((C, C), F32), ((2 * C, 2 * C), F32)], 4000 * mega,
        z, normed, scaled, factor, w_out,
    )
    back = call(
        back_kernel,
        [((32, 8 * rows, total), BF16)],
        [((total // C, 4 * total, C), F32), ((total // C, 8 * total, C), F32)], 4000 * mega,
        dedges, lr,
    )
    back = exchange(back, "dap")
    made, parts = call(
        weights_kernel,
        [((rows, 4 * C, total), BF16), ((6 * C, C), F32)],
        [((4 * C, C), BF16), ((4 * C, C), F32)], 4000 * mega,
        res_count, z, back, *sides, part_gate, part_out, smem=(0,),
    )
    share = exchange(parts.reshape(8, 96, C), "island").sum(axis=0)
    share = exchange(share.reshape(32, 3, C), "dap").sum(axis=0, keepdims=True)
    share = exchange(jnp.broadcast_to(share, (32, 3, C)), "dap").reshape(1, 96, C)
    whole = exchange(jnp.broadcast_to(share, (8, 96, C)), "island").reshape(6, C, C)
    grad = call(
        pair_kernel,
        [((1, rows, total, C), BF16)],
        [((C, 4 * C), BF16)], 4000 * mega,
        made, dgate, *sides, w_gate,
    )
    return (grad, *(whole[n] for n in range(6)))


def solution(mesh):
    rows = P("island", "dap", None, None)
    return jax.shard_map(
        on_device,
        mesh=mesh,
        in_specs=(rows, rows, P("island"), P(), P(), P(), P(), P(), P()),
        out_specs=(rows, P(), P(), P(), P(), P(), P()),
        check_vma=False,
    )
```

time: 580 us -> 289 us (0.50)
  waiting for transfers between devices: 378 us -> 62.6 us
  blocking collectives: 43.3 us -> 149 us
  matrix products: 44.3 us -> 0 us
  Pallas kernels: 0 us -> 25.3 us
  starting transfers between devices: 40.8 us -> 16.4 us
  between operations: 15.1 us -> 1.53 us
  local copies, waits for them, and re-layouts: 44.7 us -> 32.4 us
  other arithmetic: 12.1 us -> 0.07 us
    psum x1 -> x0, waiting for transfers between devices: 248 us -> none  [on_device(): lax.psum((part_left, part_lgate, part_right, part_rgate, part_gate, part_...]
    all_to_all x1 -> x5, blocking collectives: 43.3 us -> 149 us  [exchange(): return lax.all_to_all(x, axis, split_axis=0, concat_axis=0, tiled=True)]
    all_to_all x5 -> x3, waiting for transfers between devices: 130 us -> 62.6 us  [exchange(): return lax.all_to_all(x, axis, split_axis=0, concat_axis=0, tiled=True)]
    dot_general x21 -> x0, matrix products: 44.3 us -> none  [the longest x1 5.16 us: on_device(): jnp.einsum('cij,dc->ijd', right_gate_gradient, w_right_gate, preferred_el...]
    pallas_call x0 -> x8, Pallas kernels: none -> 25.3 us  [call(): pl.pallas_call(body, out_shape=shapes, in_specs=specs, out_specs=out_spec...]
    convert_element_type x12 -> x0, local copies, waits for them, and re-layouts: 24.3 us -> none  [the longest x2 5.75 us: on_device(): dlf = dleft_rows.astype(jnp.float32) * pair_residue_mask]
    all_to_all x5 -> x3, starting transfers between devices: 40.5 us -> 16.4 us  [exchange(): return lax.all_to_all(x, axis, split_axis=0, concat_axis=0, tiled=True)]
    unnamed x54 -> x76, local copies, waits for them, and re-layouts: 12.2 us -> 30.8 us
  transfers between devices with their start and end apart: 6 -> 3, of which waited for: 6 -> 3; matrix products, arithmetic and copies ran while one was open for 5% -> 0% of each run, Pallas kernels for 0% -> 3%
where the time goes in v1:
time: 289 us; the launch traced here: 287 us
  blocking collectives  149 us (52%)
  waiting for transfers between devices  62.6 us (22%)
  local copies, waits for them, and re-layouts  32.4 us (11%)
  Pallas kernels  25.3 us (9%)
  starting transfers between devices  16.4 us (6%)
    all_to_all x5, blocking collectives, exchange(): return lax.all_to_all(x, axis, split_axis=0, concat_axis=0, tiled=True)  149 us
    all_to_all x3, waiting for transfers between devices, exchange(): return lax.all_to_all(x, axis, split_axis=0, concat_axis=0, tiled=True)  62.6 us
    unnamed x76, local copies, waits for them, and re-layouts  30.8 us
    pallas_call x8, Pallas kernels, call(): pl.pallas_call(body, out_shape=shapes, in_specs=specs, out_specs=out_spec...  25.3 us
    all_to_all x3, starting transfers between devices, exchange(): return lax.all_to_all(x, axis, split_axis=0, concat_axis=0, tiled=True)  16.4 us
  transfers between devices with their start and end apart: 3, of which 3 were waited for; matrix products, arithmetic and copies ran while one was open for 0% of the time, Pallas kernels for 3%

profile of v1, /device:TPU:1, one launch (start us, length us, event | category | flops | bytes accessed | tf_op | source)
XLA Modules:
  0.0 287.1 jit_solution(1337122677098069907)
XLA Ops:
  1.3 1.3 copy-done.2
  5.6 2.6 shard_map.144
  8.2 68.1 %all_to_all.40.x_ref = bf16[32,96,384]{2,1,0:T(8,128)(2,1)S(1)} all-to-all(bf16[32,96,384]{2,1,0:T(8,128)(2,1)S(1)} %shard_map.144), channel_id=1, replica_groups=mesh['island'=8,'dap'=32] {'dap'}, dimensions={0} | all-to-all | bytes 4718592 | tf_op jit(solution)/shard_map/all_to_all | solution.py:277
  76.3 2.9 %shard_map.145 = (bf16[32,48,384]{2,1,0:T(8,128)(2,1)}, bf16[8,384,384]{2,1,0:T(8,128)(2,1)S(1)}) custom-call(bf16[32,96,384]{2,1,0:T(8,128)(2,1)S(1)} %all_to_all.40.x_ref), custom_call_target="tpu_custom_call" | custom-call | flops 4000000000 | bytes 2359296 | tf_op jit(solution)/shard_map/pallas_call | solution.py:265
  79.2 1.4 copy-done.24
  80.6 4.6 %all-to-all-start.1 = ((bf16[32,48,384]{2,1,0:T(8,128)(2,1)}), bf16[32,48,384]{2,1,0:T(8,128)(2,1)S(1)}, u32[]{:S(2)}, u32[]{:S(2)}) async-start(bf16[32,48,384]{2,1,0:T(8,128)(2,1)} %get-tuple-element.19), calls=%async_computation.1 | async-start | bytes 2359296 | tf_op jit(solution)/shard_map/all_to_all | solution.py:277
  86.8 2.9 %shard_map.146 = (bf16[6,256,384]{2,1,0:T(8,128)(2,1)S(1)}, f32[6,256,384]{2,1,0:T(8,128)S(1)}, f32[6,256,384]{2,1,0:T(8,128)S(1)}) custom-call(bf16[12,384,128]{2,1,0:T(8,128)(2,1)S(1)} %bitcast.19, bf16[12,384,128]{2,1,0:T(8,128)(2,1)S(1)} %bitcast.17, bf16[128,128]{1,0:T(8,128)(2,1)S(1)} %copy-done.18, bf16[128,128]{1,0:T(8,128)(2,1)S(1)} %copy-done.4), custom_call_target="tpu_custom_call" | custom-call | flops 4000000000 | bytes 2424832 | tf_op jit(solution)/shard_map/pallas_call | solution.py:265
  89.8 1.4 copy-done.22
  91.2 1.4 copy-done.28
  92.6 1.1 copy-done.30
  93.7 19.6 %all-to-all-done.1.e_ref = bf16[32,48,384]{2,1,0:T(8,128)(2,1)S(1)} async-done(((bf16[32,48,384]{2,1,0:T(8,128)(2,1)}), bf16[32,48,384]{2,1,0:T(8,128)(2,1)S(1)}, u32[]{:S(2)}, u32[]{:S(2)}) %all-to-all-start.1) | async-done | bytes 1179680 | tf_op jit(solution)/shard_map/all_to_all | solution.py:277
  113.3 1.7 copy-done.29
  115.0 1.7 shard_map.147
  116.7 36.8 %all_to_all.41.x_ref = bf16[32,48,384]{2,1,0:T(8,128)(2,1)S(1)} all-to-all(bf16[32,48,384]{2,1,0:T(8,128)(2,1)S(1)} %get-tuple-element.21), channel_id=1, replica_groups=mesh['island'=8,'dap'=32] {'dap'}, dimensions={0} | all-to-all | bytes 2359296 | tf_op jit(solution)/shard_map/all_to_all | solution.py:277
  153.5 2.8 shard_map.148
  156.3 1.4 copy-done
  157.7 5.1 %all-to-all-start.3 = ((bf16[32,96,384]{2,1,0:T(8,128)(2,1)}), bf16[32,96,384]{2,1,0:T(8,128)(2,1)S(1)}, u32[]{:S(2)}, u32[]{:S(2)}) async-start(bf16[32,96,384]{2,1,0:T(8,128)(2,1)} %copy-done), calls=%async_computation.3 | async-start | bytes 4718592 | tf_op jit(solution)/shard_map/all_to_all | solution.py:277
  163.6 1.7 copy-done.23
  165.2 1.3 copy-done.31
  166.5 1.3 copy-done.33
  167.8 3.0 %shard_map.149 = (bf16[6,256,384]{2,1,0:T(8,128)(2,1)S(1)}, f32[128,128]{1,0:T(8,128)S(1)}, f32[128,128]{1,0:T(8,128)S(1)}) custom-call(bf16[12,384,128]{2,1,0:T(8,128)(2,1)S(1)} %bitcast.20, bf16[6,256,384]{2,1,0:T(8,128)(2,1)S(1)} %copy-done.33, bf16[6,256,384]{2,1,0:T(8,128)(2,1)S(1)} %copy-done.31, f32[6,256,384]{2,1,0:T(8,128)S(1)} %copy-done.23, ...), custom_call_target="tpu_custom_call" | custom-call | flops 4000000000 | bytes 5931008 | tf_op jit(solution)/shard_map/pallas_call | solution.py:265
  170.8 1.0 copy-done.26
  173.1 41.2 %all-to-all-done.3.d_ref = bf16[32,96,384]{2,1,0:T(8,128)(2,1)S(1)} async-done(((bf16[32,96,384]{2,1,0:T(8,128)(2,1)}), bf16[32,96,384]{2,1,0:T(8,128)(2,1)S(1)}, u32[]{:S(2)}, u32[]{:S(2)}) %all-to-all-start.3) | async-done | bytes 2359328 | tf_op jit(solution)/shard_map/all_to_all | solution.py:277
  218.9 5.6 %shard_map.150 = (bf16[12,512,384]{2,1,0:T(8,128)(2,1)S(1)}, f32[768,128]{1,0:T(8,128)S(1)}) custom-call(s32[1]{0:T(128)S(6)} %copy.16.count_ref, bf16[12,384,128]{2,1,0:T(8,128)(2,1)S(1)} %bitcast.21, bf16[32,96,384]{2,1,0:T(8,128)(2,1)S(1)} %all-to-all-done.3.d_ref, bf16[128,128]{1,0:T(8,128)(2,1)S(1)} %copy-done.7, bf16[128,128]{1,0:T(8,128)(2,1)S(1)} %copy-done.10, ...), custom_call_target="tpu_custom_call" | custom-call | flops 4000000000 | bytes 3801092 | tf_op jit(solution)/shard_map/pallas_call | solution.py:265
  224.5 2.1 copy-done.20
  226.7 17.5 %all_to_all.42 = f32[8,96,128]{2,1,0:T(8,128)S(1)} all-to-all(f32[8,96,128]{2,1,0:T(8,128)S(1)} %bitcast.16), channel_id=1, replica_groups=mesh['island'=8,'dap'=32] {'island'}, dimensions={0} | all-to-all | bytes 786432 | tf_op jit(solution)/shard_map/all_to_all | solution.py:277
  244.2 14.5 %all_to_all.43 = f32[32,3,128]{2,1,0:T(4,128)S(1)} all-to-all(f32[32,3,128]{2,1,0:T(4,128)S(1)} %reshape.27), channel_id=1, replica_groups=mesh['island'=8,'dap'=32] {'dap'}, dimensions={0} | all-to-all | bytes 98304 | tf_op jit(solution)/shard_map/all_to_all | solution.py:277
  258.8 12.0 %all_to_all.44 = f32[32,3,128]{2,1,0:T(4,128)S(1)} all-to-all(f32[32,3,128]{2,1,0:T(4,128)S(1)} %broadcast_in_dim.6), channel_id=1, replica_groups=mesh['island'=8,'dap'=32] {'dap'}, dimensions={0} | all-to-all | bytes 98304 | tf_op jit(solution)/shard_map/all_to_all | solution.py:277
  271.6 6.7 %all-to-all-start.7 = ((f32[8,96,128]{2,1,0:T(8,128)}), f32[8,96,128]{2,1,0:T(8,128)S(1)}, u32[]{:S(2)}, u32[]{:S(2)}) async-start(f32[8,96,128]{2,1,0:T(8,128)} %broadcast_in_dim.15), calls=%async_computation.7 | async-start | bytes 786432 | tf_op jit(solution)/shard_map/all_to_all | solution.py:277
  278.4 2.3 copy-done.21
  280.7 3.9 %shard_map.151 = bf16[1,12,384,128]{3,2,1,0:T(8,128)(2,1)} custom-call(bf16[12,512,384]{2,1,0:T(8,128)(2,1)S(1)} %copy-done.21, bf16[6,256,384]{2,1,0:T(8,128)(2,1)S(1)} %copy-done.27, bf16[128,128]{1,0:T(8,128)(2,1)S(1)} %copy-done.8, bf16[128,128]{1,0:T(8,128)(2,1)S(1)} %copy-done.11, bf16[128,128]{1,0:T(8,128)(2,1)S(1)} %copy-done.14, ...), custom_call_target="tpu_custom_call" | custom-call | flops 4000000000 | bytes 6062080 | tf_op jit(solution)/shard_map/pallas_call | solution.py:265
  284.6 1.8 all-to-all-done.7
  (70 shorter events, 13.0 us)
Async XLA Ops:
  1.3 1.3 copy-start.2
  2.6 0.8 copy-start.6
  79.2 1.4 copy-start.24
  80.6 4.7 %copy-start.1 = (bf16[1,12,384,128]{3,2,1,0:T(8,128)(2,1)S(1)}, bf16[1,12,384,128]{3,2,1,0:T(8,128)(2,1)}, u32[]{:S(2)}) copy-start(bf16[1,12,384,128]{3,2,1,0:T(8,128)(2,1)} %param.10) | copy-start | bytes 3538948
  80.6 4.7 %copy-start.3 = (bf16[1,12,384,128]{3,2,1,0:T(8,128)(2,1)S(1)}, bf16[1,12,384,128]{3,2,1,0:T(8,128)(2,1)}, u32[]{:S(2)}) copy-start(bf16[1,12,384,128]{3,2,1,0:T(8,128)(2,1)} %param.9) | copy-start | bytes 3538948
  80.6 32.7 %all-to-all-start.1 = ((bf16[32,48,384]{2,1,0:T(8,128)(2,1)}), bf16[32,48,384]{2,1,0:T(8,128)(2,1)S(1)}, u32[]{:S(2)}, u32[]{:S(2)}) async-start(bf16[32,48,384]{2,1,0:T(8,128)(2,1)} %get-tuple-element.19), calls=%async_computation.1 | async-start | bytes 2359296 | tf_op jit(solution)/shard_map/all_to_all | solution.py:277
  85.3 0.8 copy-start.4
  89.8 1.4 copy-start.22
  91.2 1.4 copy-start.28
  92.6 1.1 copy-start.30
  113.3 1.7 copy-start.29
  116.7 36.9 %copy-start.32 = (bf16[6,256,384]{2,1,0:T(8,128)(2,1)}, bf16[6,256,384]{2,1,0:T(8,128)(2,1)S(1)}, u32[]{:S(2)}) copy-start(bf16[6,256,384]{2,1,0:T(8,128)(2,1)S(1)} %get-tuple-element.23.nm_ref) | copy-start | bytes 3538948
  116.7 36.8 %copy-start.25 = (bf16[8,384,384]{2,1,0:T(8,128)(2,1)S(1)}, bf16[8,384,384]{2,1,0:T(8,128)(2,1)}, u32[]{:S(2)}) copy-start(bf16[8,384,384]{2,1,0:T(8,128)(2,1)} %copy-done.24) | copy-start | bytes 7077892
  156.3 1.4 copy-start
  157.7 56.5 %all-to-all-start.3 = ((bf16[32,96,384]{2,1,0:T(8,128)(2,1)}), bf16[32,96,384]{2,1,0:T(8,128)(2,1)S(1)}, u32[]{:S(2)}, u32[]{:S(2)}) async-start(bf16[32,96,384]{2,1,0:T(8,128)(2,1)} %copy-done), calls=%async_computation.3 | async-start | bytes 4718592 | tf_op jit(solution)/shard_map/all_to_all | solution.py:277
  162.8 0.8 copy-start.5
  163.6 1.7 copy-start.23
  165.2 1.3 copy-start.31
  166.5 1.3 copy-start.33
  170.8 1.0 copy-start.26
  214.2 0.8 copy-start.7
  217.2 0.8 copy-start.35
  218.1 0.8 copy-start.37
  224.5 2.1 copy-start.20
  244.1 34.2 %copy-start.8 = (bf16[128,128]{1,0:T(8,128)(2,1)S(1)}, bf16[128,128]{1,0:T(8,128)(2,1)}, u32[]{:S(2)}) copy-start(bf16[128,128]{1,0:T(8,128)(2,1)} %wl_ref.5) | copy-start | bytes 98308
  244.1 34.2 %copy-start.11 = (bf16[128,128]{1,0:T(8,128)(2,1)S(1)}, bf16[128,128]{1,0:T(8,128)(2,1)}, u32[]{:S(2)}) copy-start(bf16[128,128]{1,0:T(8,128)(2,1)} %wlg_ref.5) | copy-start | bytes 98308
  244.1 34.2 %copy-start.14 = (bf16[128,128]{1,0:T(8,128)(2,1)S(1)}, bf16[128,128]{1,0:T(8,128)(2,1)}, u32[]{:S(2)}) copy-start(bf16[128,128]{1,0:T(8,128)(2,1)} %wr_ref.5) | copy-start | bytes 98308
  244.1 34.2 %copy-start.17 = (bf16[128,128]{1,0:T(8,128)(2,1)S(1)}, bf16[128,128]{1,0:T(8,128)(2,1)}, u32[]{:S(2)}) copy-start(bf16[128,128]{1,0:T(8,128)(2,1)} %wrg_ref.5) | copy-start | bytes 98308
  244.1 34.2 %copy-start.19 = (bf16[128,128]{1,0:T(8,128)(2,1)S(1)}, bf16[128,128]{1,0:T(8,128)(2,1)}, u32[]{:S(2)}) copy-start(bf16[128,128]{1,0:T(8,128)(2,1)} %wg_ref.3) | copy-start | bytes 98308
  244.1 34.2 %copy-start.27 = (bf16[6,256,384]{2,1,0:T(8,128)(2,1)S(1)}, bf16[6,256,384]{2,1,0:T(8,128)(2,1)}, u32[]{:S(2)}) copy-start(bf16[6,256,384]{2,1,0:T(8,128)(2,1)} %copy-done.26) | copy-start | bytes 3538948
  271.6 14.8 %all-to-all-start.7 = ((f32[8,96,128]{2,1,0:T(8,128)}), f32[8,96,128]{2,1,0:T(8,128)S(1)}, u32[]{:S(2)}, u32[]{:S(2)}) async-start(f32[8,96,128]{2,1,0:T(8,128)} %broadcast_in_dim.15), calls=%async_computation.7 | async-start | bytes 786432 | tf_op jit(solution)/shard_map/all_to_all | solution.py:277
  278.3 2.3 copy-start.21
  (9 other events, 6.6 us)

commit v2 on v1

v2 whole, which is shorter than its diff:
```python
import jax
import jax.numpy as jnp
from jax import lax
from jax.experimental import pallas as pl
from jax.experimental.pallas import tpu as pltpu
from jax.sharding import Mesh
from jax.sharding import PartitionSpec as P

F32 = jnp.float32
BF16 = jnp.bfloat16
C = 128
HI = lax.Precision.HIGHEST
ISLAND, DAP = ("x", "core"), ("z", "y")


def dot(a, b, ca, cb, precision=None):
    return lax.dot_general(
        a, b, (((ca,), (cb,)), ((), ())), preferred_element_type=F32, precision=precision
    )


def iota(shape, dim):
    return lax.broadcasted_iota(jnp.int32, shape, dim)


def pick(side):
    row, chan = iota((2 * C, C), 0), iota((2 * C, C), 1)
    hit = ((row % 8) // 4 == side) & (chan == (row // 8) * 4 + row % 4)
    return hit.astype(F32)


def spread_rows(w_out):
    parts = [dot(pick(side).astype(BF16), w_out, 1, 0) for side in range(2)]
    return jnp.concatenate(parts, axis=1).astype(BF16)


def both_projections(w_left, w_left_gate, w_right, w_right_gate):
    on_left, on_right = pick(0).astype(BF16), pick(1).astype(BF16)
    proj = dot(on_left, w_left, 1, 1) + dot(on_right, w_right, 1, 1)
    gate = dot(on_left, w_left_gate, 1, 1) + dot(on_right, w_right_gate, 1, 1)
    return jnp.concatenate([proj, gate], axis=0).astype(BF16)


def row_mask(count, row, shape):
    return jnp.where((row < count) & (iota(shape, len(shape) - 1) < count), 1.0, 0.0)


def first_row(rows):
    return lax.axis_index(DAP) * rows


def each(n, step):
    def body(m, carry):
        step(m)
        return carry

    lax.fori_loop(0, n, body, 0)


def two(m):
    return pl.ds(2 * m, 2)


def tile(m):
    return pl.ds(pl.multiple_of(16 * m, 16), 16)


def project_kernel(
    count_ref, z_hbm, wl_hbm, wlg_hbm, wr_hbm, wrg_hbm, out_hbm,
    w_ref, z_ref, side_ref, out_ref, z_sem, w_sem, out_sem,
):
    rows, total, _ = z_ref.shape
    count = count_ref[0]
    start = first_row(rows)
    sides = [
        pltpu.make_async_copy(ref, side_ref.at[n], w_sem.at[n])
        for n, ref in enumerate((wl_hbm, wlg_hbm, wr_hbm, wrg_hbm))
    ]
    for copy in sides:
        copy.start()

    def cells(m):
        return pltpu.make_async_copy(z_hbm.at[two(m)], z_ref.at[two(m)], z_sem.at[m])

    def sent(m):
        return pltpu.make_async_copy(out_ref.at[:, tile(m)], out_hbm.at[:, tile(m)], out_sem.at[m])

    each(rows // 2, lambda m: cells(m).start())
    for copy in sides:
        copy.wait()
    w_ref[...] = both_projections(side_ref[0], side_ref[1], side_ref[2], side_ref[3])

    def step(m):
        cells(m).wait()
        halves = []
        for h in range(2):
            i = 2 * m + h
            pg = dot(w_ref[...], z_ref[i], 1, 1)
            mask = row_mask(count, start + i, (1, total))
            made = mask * jax.nn.sigmoid(pg[2 * C :]) * pg[: 2 * C]
            halves.append(made.reshape(32, 8, total))
        out_ref[:, tile(m), :] = jnp.concatenate(halves, axis=1).astype(BF16)
        sent(m).start()

    each(rows // 2, step)
    each(rows // 2, lambda m: sent(m).wait())


def factors_kernel(count_ref, z_ref, wl_ref, wlg_ref, wr_ref, wrg_ref, out_ref, w_ref):
    rows, total, _ = z_ref.shape
    count = count_ref[0]
    start = first_row(rows)
    w_ref[...] = both_projections(wl_ref[...], wlg_ref[...], wr_ref[...], wrg_ref[...])

    def body(i, carry):
        pg = dot(w_ref[...], z_ref[i], 1, 1)
        gate = jax.nn.sigmoid(pg[2 * C :])
        masked = gate * row_mask(count, start + i, (1, total))
        out_ref[i, : 2 * C, :] = masked.astype(BF16)
        out_ref[i, 2 * C :, :] = (masked * pg[: 2 * C] * (1.0 - gate)).astype(BF16)
        return carry

    lax.fori_loop(0, rows, body, 0)


def put_wide(ref, at, rows, value):
    for n in range(ref.shape[0]):
        ref[n, pl.ds(at, rows), :] = value[:, n * C : (n + 1) * C]


def take(ref, first, count, step):
    return jnp.concatenate(
        [ref[n, pl.ds(first, count, stride=step), :] for n in range(ref.shape[0])], axis=1
    )


def put(ref, first, count, step, value):
    for n in range(ref.shape[0]):
        ref[n, pl.ds(first, count, stride=step), :] = value[:, n * C : (n + 1) * C]


def get_rows(ref, at, rows):
    return jnp.concatenate([ref[n, pl.ds(at, rows), :] for n in range(ref.shape[0])], axis=1)


def widen_all(x_hbm, x_ref, wide_ref, sem):
    devices, block, _ = x_ref.shape
    part = devices // 4

    def copy(n):
        here = pl.ds(n * part, part)
        return pltpu.make_async_copy(x_hbm.at[here], x_ref.at[here], sem.at[n])

    def widen(s):
        put_wide(wide_ref, pl.multiple_of(s * block, block), block, x_ref[s].astype(F32))

    def step(n):
        copy(n).wait()
        each(part, lambda s: widen(n * part + s))

    return lambda: each(4, lambda n: copy(n).start()), lambda: each(4, step)


def edges_kernel(x_hbm, out_hbm, lr_hbm, wide_ref, prod_ref, lr_ref, x_ref, out_ref, lr_sem, x_sem, out_sem):
    total = x_ref.shape[2]
    fetch, widen = widen_all(x_hbm, x_ref, wide_ref, x_sem)
    fetch()
    widen()

    def kept(c):
        return pltpu.make_async_copy(lr_ref.at[two(c)], lr_hbm.at[two(c)], lr_sem.at[c])

    for c in range(4):
        left = take(wide_ref, c, total, 8).astype(BF16)
        right = take(wide_ref, 4 + c, total, 8).astype(BF16)
        lr_ref[2 * c] = left
        lr_ref[2 * c + 1] = right
        kept(c).start()
        put(prod_ref, c, total, 4, dot(left, right, 1, 1))
    for copy in narrowed(prod_ref, out_ref, out_hbm, out_sem):
        copy.wait()
    each(4, lambda c: kept(c).wait())


def narrowed(prod_ref, out_ref, out_hbm, sem):
    devices, block, _ = out_ref.shape
    part = devices // 4
    copies = []
    for n in range(4):

        def narrow(s, carry):
            at = pl.multiple_of(s * block, block)
            out_ref[s] = get_rows(prod_ref, at, block).astype(BF16)
            return carry

        lax.fori_loop(n * part, (n + 1) * part, narrow, 0)
        here = pl.ds(n * part, part)
        copies.append(pltpu.make_async_copy(out_ref.at[here], out_hbm.at[here], sem.at[n]))
        copies[-1].start()
    return copies


def gates_kernel(z_ref, g_ref, wg_ref, wo_ref, ds_ref, fac_ref, dn_ref, wgt_ref, wx_ref):
    rows = z_ref.shape[0]
    wgt_ref[...] = wg_ref[...].astype(F32).T.astype(BF16)
    wx_ref[...] = spread_rows(wo_ref[...])

    def body(m, carry):
        for h in range(2):
            i = 2 * m + h
            gate = jax.nn.sigmoid(dot(wgt_ref[...], z_ref[i], 1, 1))
            scaled = g_ref[i].astype(F32).T * gate
            ds_ref[m, h * C : (h + 1) * C, :] = scaled.astype(BF16)
            fac_ref[m, h * C : (h + 1) * C, :] = scaled * (1.0 - gate)
        dn_ref[m] = dot(wx_ref[...], ds_ref[m], 1, 0)
        return carry

    lax.fori_loop(0, rows // 2, body, 0)


def chan_mean(x):
    s = jnp.sum(x, axis=0)
    top = iota(s.shape, 0) < 4
    first = jnp.sum(jnp.where(top, s, 0.0), axis=0, keepdims=True)
    second = jnp.sum(jnp.where(top, 0.0, s), axis=0, keepdims=True)
    return jnp.where(top, first, second) * (1.0 / C)


def norm_kernel(
    count_ref, e_hbm, dn_hbm, de_hbm, nm_hbm, e_ref, dn_ref, de_ref, nm_ref, e_sem, dn_sem, de_sem, nm_sem
):
    devices, block, total = e_ref.shape
    rows = block // 4
    count = count_ref[0]
    start = first_row(rows)

    def came(q):
        return (
            pltpu.make_async_copy(e_hbm.at[:, tile(q)], e_ref.at[:, tile(q)], e_sem.at[q]),
            pltpu.make_async_copy(dn_hbm.at[two(q)], dn_ref.at[two(q)], dn_sem.at[q]),
        )

    def gone(q):
        return (
            pltpu.make_async_copy(de_ref.at[:, tile(q)], de_hbm.at[:, tile(q)], de_sem.at[q]),
            pltpu.make_async_copy(nm_ref.at[two(q)], nm_hbm.at[two(q)], nm_sem.at[q]),
        )

    def begin(q):
        for copy in came(q):
            copy.start()

    def finish(q):
        for copy in gone(q):
            copy.wait()

    def step(q):
        for copy in came(q):
            copy.wait()
        e_all = e_ref[:, tile(q), :].astype(F32)
        halves = []
        for h in range(2):
            e = e_all[:, 8 * h : 8 * h + 8, :]
            row = start + 4 * q + 2 * h + iota((8, total), 0) // 4
            mask = row_mask(count, row, (8, total))
            shifted = e - chan_mean(e)[None]
            rs = lax.rsqrt(chan_mean(shifted * shifted) + 1e-05)
            xhat = shifted * rs[None]
            nm_ref[2 * q + h] = (xhat * mask[None]).reshape(2 * C, total).astype(BF16)
            dn = dn_ref[2 * q + h].reshape(32, 8, total)
            m1 = chan_mean(dn)
            m2 = chan_mean(dn * xhat)
            halves.append((mask * rs)[None] * (dn - m1[None] - xhat * m2[None]))
        de_ref[:, tile(q), :] = jnp.concatenate(halves, axis=1).astype(BF16)
        for copy in gone(q):
            copy.start()

    each(rows // 4, begin)
    each(rows // 4, step)
    each(rows // 4, finish)


def linear_kernel(z_ref, nm_ref, ds_ref, fac_ref, wo_ref, dg_ref, sums_ref, wx_ref, ga_ref, oa_ref):
    rows = z_ref.shape[0]
    wx_ref[...] = spread_rows(wo_ref[...]).astype(F32).T.astype(BF16)
    ga_ref[...] = jnp.zeros_like(ga_ref)
    oa_ref[...] = jnp.zeros_like(oa_ref)

    def body(m, carry):
        lin = dot(wx_ref[...], nm_ref[m], 1, 0)
        dg_ref[m] = (lin * fac_ref[m]).astype(BF16)
        for h in range(2):
            ga_ref[...] += dot(dg_ref[m, h * C : (h + 1) * C, :], z_ref[2 * m + h], 1, 0)
        oa_ref[...] += dot(nm_ref[m], ds_ref[m], 1, 1)
        return carry

    lax.fori_loop(0, rows // 2, body, 0)
    sums_ref[:C, :] = ga_ref[...].T
    sums_ref[C:, :] = dot(pick(0), oa_ref[:, :C], 0, 0, HI) + dot(pick(1), oa_ref[:, C:], 0, 0, HI)


def back_kernel(x_hbm, lr_hbm, out_hbm, wide_ref, prod_ref, lr_ref, x_ref, out_ref, lr_sem, x_sem, out_sem):
    total = x_ref.shape[2]

    def kept(c):
        return pltpu.make_async_copy(lr_hbm.at[two(c)], lr_ref.at[two(c)], lr_sem.at[c])

    fetch, widen = widen_all(x_hbm, x_ref, wide_ref, x_sem)
    fetch()
    each(4, lambda c: kept(c).start())
    widen()
    for c in range(4):
        de = take(wide_ref, c, total, 4)
        kept(c).wait()
        put(prod_ref, c, total, 8, dot(de.astype(BF16), lr_ref[2 * c + 1], 1, 0))
        put(prod_ref, 4 + c, total, 8, dot(de.T.astype(BF16), lr_ref[2 * c], 1, 0))
    for copy in narrowed(prod_ref, out_ref, out_hbm, out_sem):
        copy.wait()


def by_side(x):
    x = x.reshape(16, 2, 8, C)
    even, odd = x[:, 0], x[:, 1]
    top = iota((16, 8, C), 1) < 4
    left = jnp.where(top, even, pltpu.roll(odd, 4, 1))
    right = jnp.where(top, pltpu.roll(even, 4, 1), odd)
    return left.reshape(C, C), right.reshape(C, C)


def side_gradients(d_ref, fac_ref, m, h):
    d = d_ref[:, tile(m), :].astype(F32)[:, 8 * h : 8 * h + 8, :].reshape(2 * C, -1)
    factor = fac_ref[2 * m + h].astype(F32)
    return jnp.concatenate([d * factor[: 2 * C], d * factor[2 * C :]], axis=0).astype(BF16)


def weights_kernel(
    z_hbm, d_hbm, fac_hbm, sums_hbm, out_ref, acc_ref, z_ref, d_ref, fac_ref, z_sem, d_sem, fac_sem, sums_sem
):
    rows, total, _ = z_ref.shape

    def came(m):
        return (
            pltpu.make_async_copy(d_hbm.at[:, tile(m)], d_ref.at[:, tile(m)], d_sem.at[m]),
            pltpu.make_async_copy(fac_hbm.at[two(m)], fac_ref.at[two(m)], fac_sem.at[m]),
            pltpu.make_async_copy(z_hbm.at[two(m)], z_ref.at[two(m)], z_sem.at[m]),
        )

    def begin(m):
        for copy in came(m):
            copy.start()

    def step(m):
        for copy in came(m):
            copy.wait()
        for h in range(2):
            acc_ref[...] += dot(side_gradients(d_ref, fac_ref, m, h), z_ref[2 * m + h], 1, 0)

    each(rows // 2, begin)
    rest = pltpu.make_async_copy(sums_hbm, out_ref.at[pl.ds(4 * C, 2 * C)], sums_sem.at[0])
    rest.start()
    acc_ref[...] = jnp.zeros_like(acc_ref)
    each(rows // 2, step)
    for n in range(2):
        left, right = by_side(acc_ref[2 * C * n : 2 * C * (n + 1), :])
        out_ref[n * C : (n + 1) * C, :] = left.T
        out_ref[(2 + n) * C : (3 + n) * C, :] = right.T
    rest.wait()


def pair_kernel(d_ref, fac_ref, dg_ref, w_ref, wg_ref, out_ref, wt_ref):
    rows = fac_ref.shape[0]
    wt_ref[...] = w_ref[...].astype(F32).T.astype(BF16)

    def body(m, carry):
        for h in range(2):
            i = 2 * m + h
            made = dot(wt_ref[...], side_gradients(d_ref, fac_ref, m, h), 1, 0)
            made += dot(wg_ref[...], dg_ref[m, h * C : (h + 1) * C, :], 1, 0)
            out_ref[0, i] = made.T.astype(BF16)
        return carry

    lax.fori_loop(0, rows // 2, body, 0)


def call(body, outs, scratch, flops, *args, smem=(), hbm=(), hbm_out=(), sems=()):
    spaces = [pltpu.SMEM if n in smem else pltpu.HBM if n in hbm else pltpu.VMEM for n in range(len(args))]
    shapes = [jax.ShapeDtypeStruct(s, t) for s, t in outs]
    out_specs = [
        pl.BlockSpec(memory_space=pltpu.HBM if n in hbm_out else pltpu.VMEM) for n in range(len(outs))
    ]
    if len(outs) == 1:
        shapes, out_specs = shapes[0], out_specs[0]
    moved = sum(a.size * a.dtype.itemsize for a in args)
    return pl.pallas_call(
        body,
        out_shape=shapes,
        in_specs=[pl.BlockSpec(memory_space=space) for space in spaces],
        out_specs=out_specs,
        scratch_shapes=[pltpu.VMEM(s, t) for s, t in scratch] + [pltpu.SemaphoreType.DMA((n,)) for n in sems],
        compiler_params=pltpu.CompilerParams(vmem_limit_bytes=62 << 20),
        cost_estimate=pl.CostEstimate(flops=flops, bytes_accessed=moved, transcendentals=0),
    )(*args)


def exchange(x, axis):
    return lax.all_to_all(x, axis, split_axis=0, concat_axis=0, tiled=True)


def on_device(
    pair, cotangent, res_count, w_left, w_left_gate, w_right, w_right_gate, w_gate, w_out
):
    z, g = pair[0], cotangent[0]
    rows, total, _ = z.shape
    pairs = rows // 2
    sides = (w_left, w_left_gate, w_right, w_right_gate)
    mega = 10**6

    blocks = call(
        project_kernel, [((32, 8 * rows, total), BF16)],
        [((4 * C, C), BF16), ((rows, total, C), BF16), ((4, C, C), BF16), ((32, 8 * rows, total), BF16)],
        4000 * mega, res_count, z, *sides, smem=(0,), hbm=(1, 2, 3, 4, 5), hbm_out=(0,), sems=(pairs, 4, pairs),
    )
    blocks = exchange(blocks, DAP)
    factors, w_all = call(
        factors_kernel, [((rows, 4 * C, total), BF16), ((4 * C, C), BF16)], [], 4000 * mega,
        res_count, z, *sides, smem=(0,),
    )
    scaled, factor, dnormed = call(
        gates_kernel,
        [((pairs, 2 * C, total), BF16), ((pairs, 2 * C, total), F32), ((pairs, 2 * C, total), F32)],
        [((C, C), BF16), ((2 * C, 2 * C), BF16)], 4000 * mega,
        z, g, w_gate, w_out,
    )
    edges, lr = call(
        edges_kernel,
        [((32, 4 * rows, total), BF16), ((8, total, total), BF16)],
        [
            ((total // C, 8 * total, C), F32), ((total // C, 4 * total, C), F32),
            ((8, total, total), BF16), ((32, 8 * rows, total), BF16), ((32, 4 * rows, total), BF16),
        ], 4000 * mega,
        blocks, hbm=(0,), hbm_out=(0, 1), sems=(4, 4, 4),
    )
    edges = exchange(edges, DAP)
    dedges, normed = call(
        norm_kernel,
        [((32, 4 * rows, total), BF16), ((pairs, 2 * C, total), BF16)],
        [
            ((32, 4 * rows, total), BF16), ((pairs, 2 * C, total), F32),
            ((32, 4 * rows, total), BF16), ((pairs, 2 * C, total), BF16),
        ], 4000 * mega,
        res_count, edges, dnormed, smem=(0,), hbm=(1, 2), hbm_out=(0, 1), sems=(rows // 4,) * 4,
    )
    dedges = exchange(dedges, DAP)
    dgate, sums = call(
        linear_kernel,
        [((pairs, 2 * C, total), BF16), ((2 * C, C), F32)],
        [((2 * C, 2 * C), BF16), ((C, C), F32), ((2 * C, 2 * C), F32)], 4000 * mega,
        z, normed, scaled, factor, w_out,
    )
    back = call(
        back_kernel,
        [((32, 8 * rows, total), BF16)],
        [
            ((total // C, 4 * total, C), F32), ((total // C, 8 * total, C), F32),
            ((8, total, total), BF16), ((32, 4 * rows, total), BF16), ((32, 8 * rows, total), BF16),
        ], 4000 * mega,
        dedges, lr, hbm=(0, 1), hbm_out=(0,), sems=(4, 4, 4),
    )
    back = exchange(back, DAP)
    parts = call(
        weights_kernel,
        [((6 * C, C), F32)],
        [
            ((4 * C, C), F32), ((rows, total, C), BF16),
            ((32, 8 * rows, total), BF16), ((rows, 4 * C, total), BF16),
        ], 4000 * mega,
        z, back, factors, sums, hbm=(0, 1, 2, 3), sems=(pairs, pairs, pairs, 1),
    )
    near = ("x", "core", "y")
    share = exchange(parts.reshape(32, 24, C), near).sum(axis=0, keepdims=True)
    share = exchange(jnp.broadcast_to(share, (8, 24, C)), "z").sum(axis=0, keepdims=True)
    whole = exchange(jnp.broadcast_to(share, (32, 24, C)), near).reshape(6, C, C)
    grad = call(
        pair_kernel,
        [((1, rows, total, C), BF16)],
        [((C, 4 * C), BF16)], 4000 * mega,
        back, factors, dgate, w_all, w_gate,
    )
    return (grad, *(whole[n] for n in range(6)))


def solution(mesh):
    chips = Mesh(mesh.devices.reshape(4, 2, 8, 4), ISLAND + DAP)
    rows = P(ISLAND, DAP, None, None)
    return jax.shard_map(
        on_device,
        mesh=chips,
        in_specs=(rows, rows, P(ISLAND), P(), P(), P(), P(), P(), P()),
        out_specs=(rows, P(), P(), P(), P(), P(), P()),
        check_vma=False,
    )
```

time: 289 us -> 271 us (0.938)
  local copies, waits for them, and re-layouts: 32.4 us -> 2.57 us
  Pallas kernels: 25.3 us -> 51.3 us
  blocking collectives: 149 us -> 138 us
    unnamed x76 -> x2, local copies, waits for them, and re-layouts: 30.8 us -> 1.01 us
    pallas_call x8 -> x9, Pallas kernels: 25.3 us -> 51.3 us  [call(): pl.pallas_call(body, out_shape=shapes, in_specs=[pl.BlockSpec(memory_spac...]
    all_to_all x5 -> x4, blocking collectives: 149 us -> 138 us  [exchange(): return lax.all_to_all(x, axis, split_axis=0, concat_axis=0, tiled=True)]
  transfers between devices with their start and end apart: 3 -> 3, of which waited for: 3 -> 3; matrix products, arithmetic and copies ran while one was open for 0% -> 0% of each run, Pallas kernels for 3% -> 10%
where the time goes in v2:
time: 271 us; the launch traced here: 270 us
  blocking collectives  138 us (51%)
  waiting for transfers between devices  61.6 us (23%)
  Pallas kernels  51.3 us (19%)
  starting transfers between devices  15.3 us (6%)
    all_to_all x4, blocking collectives, exchange(): return lax.all_to_all(x, axis, split_axis=0, concat_axis=0, tiled=True)  138 us
    all_to_all x3, waiting for transfers between devices, exchange(): return lax.all_to_all(x, axis, split_axis=0, concat_axis=0, tiled=True)  61.6 us
    pallas_call x9, Pallas kernels, call(): pl.pallas_call(body, out_shape=shapes, in_specs=[pl.BlockSpec(memory_spac...  51.3 us
    all_to_all x3, starting transfers between devices, exchange(): return lax.all_to_all(x, axis, split_axis=0, concat_axis=0, tiled=True)  15.3 us
  transfers between devices with their start and end apart: 3, of which 3 were waited for; matrix products, arithmetic and copies ran while one was open for 0% of the time, Pallas kernels for 10%

profile of v2, /device:TPU:1, one launch (start us, length us, event | category | flops | bytes accessed | tf_op | source)
XLA Modules:
  0.0 270.3 jit_solution(11173289535447484685)
XLA Ops:
  1.3 4.3 %shard_map.144 = bf16[32,96,384]{2,1,0:T(8,128)(2,1)} custom-call(s32[1]{0:T(128)S(6)} %copy.16.count_ref, bf16[12,384,128]{2,1,0:T(8,128)(2,1)} %bitcast.19, bf16[128,128]{1,0:T(8,128)(2,1)} %wl_ref.1, bf16[128,128]{1,0:T(8,128)(2,1)} %wlg_ref.1, bf16[128,128]{1,0:T(8,128)(2,1)} %wr_ref.1, bf16[128,128]{1,0:T(8,128)(2,1)} %wrg_ref.1), custom_call_target="tpu_custom_call" | custom-call | flops 4000000000 | bytes 1310724 | tf_op jit(solution)/shard_map/pallas_call | solution.py:394
  5.6 68.4 %all_to_all.35.x_hbm = bf16[32,96,384]{2,1,0:T(8,128)(2,1)} all-to-all(bf16[32,96,384]{2,1,0:T(8,128)(2,1)} %shard_map.144), channel_id=1, replica_groups=mesh['x'=4,'core'=2,'z'=8,'y'=4] {'z','y'}, dimensions={0} | all-to-all | bytes 4718592 | tf_op jit(solution)/shard_map/all_to_all | solution.py:406
  74.0 4.6 %shard_map.145 = (bf16[32,48,384]{2,1,0:T(8,128)(2,1)}, bf16[8,384,384]{2,1,0:T(8,128)(2,1)}) custom-call(bf16[32,96,384]{2,1,0:T(8,128)(2,1)} %all_to_all.35.x_hbm), custom_call_target="tpu_custom_call" | custom-call | flops 4000000000 | bytes 2359296 | tf_op jit(solution)/shard_map/pallas_call | solution.py:394
  78.6 4.5 %all-to-all-start.1 = ((bf16[32,48,384]{2,1,0:T(8,128)(2,1)}), bf16[32,48,384]{2,1,0:T(8,128)(2,1)S(1)}, u32[]{:S(2)}, u32[]{:S(2)}) async-start(bf16[32,48,384]{2,1,0:T(8,128)(2,1)} %get-tuple-element.18), calls=%async_computation.1 | async-start | bytes 2359296 | tf_op jit(solution)/shard_map/all_to_all | solution.py:406
  83.1 6.8 %shard_map.146 = (bf16[6,256,384]{2,1,0:T(8,128)(2,1)}, f32[6,256,384]{2,1,0:T(8,128)}, f32[6,256,384]{2,1,0:T(8,128)}) custom-call(bf16[12,384,128]{2,1,0:T(8,128)(2,1)} %bitcast.20, bf16[12,384,128]{2,1,0:T(8,128)(2,1)} %bitcast.18, bf16[128,128]{1,0:T(8,128)(2,1)} %wg_ref.3, bf16[128,128]{1,0:T(8,128)(2,1)} %wo_ref.3), custom_call_target="tpu_custom_call" | custom-call | flops 4000000000 | bytes 2424832 | tf_op jit(solution)/shard_map/pallas_call | solution.py:394
  90.0 21.2 %all-to-all-done.1.e_hbm = bf16[32,48,384]{2,1,0:T(8,128)(2,1)S(1)} async-done(((bf16[32,48,384]{2,1,0:T(8,128)(2,1)}), bf16[32,48,384]{2,1,0:T(8,128)(2,1)S(1)}, u32[]{:S(2)}, u32[]{:S(2)}) %all-to-all-start.1) | async-done | bytes 1179680 | tf_op jit(solution)/shard_map/all_to_all | solution.py:406
  111.2 0.0 copy-start
  111.2 1.0 copy-done
  112.2 3.8 %shard_map.147 = (bf16[32,48,384]{2,1,0:T(8,128)(2,1)}, bf16[6,256,384]{2,1,0:T(8,128)(2,1)}) custom-call(s32[1]{0:T(128)S(6)} %copy.16.count_ref, bf16[32,48,384]{2,1,0:T(8,128)(2,1)} %copy-done, f32[6,256,384]{2,1,0:T(8,128)} %get-tuple-element.19.dn_hbm), custom_call_target="tpu_custom_call" | custom-call | flops 4000000000 | bytes 3538948 | tf_op jit(solution)/shard_map/pallas_call | solution.py:394
  116.0 36.8 %all_to_all.36.x_hbm = bf16[32,48,384]{2,1,0:T(8,128)(2,1)} all-to-all(bf16[32,48,384]{2,1,0:T(8,128)(2,1)} %get-tuple-element.20), channel_id=1, replica_groups=mesh['x'=4,'core'=2,'z'=8,'y'=4] {'z','y'}, dimensions={0} | all-to-all | bytes 2359296 | tf_op jit(solution)/shard_map/all_to_all | solution.py:406
  152.8 5.8 %shard_map.148 = bf16[32,96,384]{2,1,0:T(8,128)(2,1)} custom-call(bf16[32,48,384]{2,1,0:T(8,128)(2,1)} %all_to_all.36.x_hbm, bf16[8,384,384]{2,1,0:T(8,128)(2,1)} %get-tuple-element.21.lr_hbm), custom_call_target="tpu_custom_call" | custom-call | flops 4000000000 | bytes 3538944 | tf_op jit(solution)/shard_map/pallas_call | solution.py:394
  158.7 5.2 %all-to-all-start.3 = ((bf16[32,96,384]{2,1,0:T(8,128)(2,1)}), bf16[32,96,384]{2,1,0:T(8,128)(2,1)}, u32[]{:S(2)}, u32[]{:S(2)}) async-start(bf16[32,96,384]{2,1,0:T(8,128)(2,1)} %shard_map.148), calls=%async_computation.3 | async-start | bytes 4718592 | tf_op jit(solution)/shard_map/all_to_all | solution.py:406
  163.8 7.5 %shard_map.149 = (bf16[12,512,384]{2,1,0:T(8,128)(2,1)}, bf16[512,128]{1,0:T(8,128)(2,1)}) custom-call(s32[1]{0:T(128)S(6)} %copy.16.count_ref, bf16[12,384,128]{2,1,0:T(8,128)(2,1)} %bitcast.21, bf16[128,128]{1,0:T(8,128)(2,1)} %wl_ref.1, bf16[128,128]{1,0:T(8,128)(2,1)} %wlg_ref.1, bf16[128,128]{1,0:T(8,128)(2,1)} %wr_ref.1, bf16[128,128]{1,0:T(8,128)(2,1)} %wrg_ref.1), custom_call_target="tpu_custom_call" | custom-call | flops 4000000000 | bytes 1310724 | tf_op jit(solution)/shard_map/pallas_call | solution.py:394
  171.4 6.3 %shard_map.150 = (bf16[6,256,384]{2,1,0:T(8,128)(2,1)}, f32[256,128]{1,0:T(8,128)}) custom-call(bf16[12,384,128]{2,1,0:T(8,128)(2,1)} %bitcast.22, bf16[6,256,384]{2,1,0:T(8,128)(2,1)} %get-tuple-element.23.nm_ref, bf16[6,256,384]{2,1,0:T(8,128)(2,1)} %get-tuple-element.24.ds_ref, f32[6,256,384]{2,1,0:T(8,128)} %get-tuple-element.25.fac_ref, ...), custom_call_target="tpu_custom_call" | custom-call | flops 4000000000 | bytes 5931008 | tf_op jit(solution)/shard_map/pallas_call | solution.py:394
  177.7 37.5 %all-to-all-done.3.d_ref.d_hbm = bf16[32,96,384]{2,1,0:T(8,128)(2,1)} async-done(((bf16[32,96,384]{2,1,0:T(8,128)(2,1)}), bf16[32,96,384]{2,1,0:T(8,128)(2,1)}, u32[]{:S(2)}, u32[]{:S(2)}) %all-to-all-start.3) | async-done | bytes 2359328 | tf_op jit(solution)/shard_map/all_to_all | solution.py:406
  215.3 4.7 %shard_map.152 = f32[768,128]{1,0:T(8,128)} custom-call(bf16[12,384,128]{2,1,0:T(8,128)(2,1)} %bitcast.23, bf16[32,96,384]{2,1,0:T(8,128)(2,1)} %all-to-all-done.3.d_ref.d_hbm, bf16[12,512,384]{2,1,0:T(8,128)(2,1)} %get-tuple-element.22.fac_ref.fac_hbm, f32[256,128]{1,0:T(8,128)} %get-tuple-element.28.sums_hbm), custom_call_target="tpu_custom_call" | custom-call | flops 4000000000 | bytes 8388608 | tf_op jit(solution)/shard_map/pallas_call | solution.py:394
  220.0 22.6 %all_to_all.37 = f32[32,24,128]{2,1,0:T(8,128)S(1)} all-to-all(f32[32,24,128]{2,1,0:T(8,128)} %bitcast.17), channel_id=1, replica_groups=mesh['x'=4,'core'=2,'z'=8,'y'=4] {'x','core','y'}, dimensions={0} | all-to-all | bytes 786432 | tf_op jit(solution)/shard_map/all_to_all | solution.py:406
  242.6 10.4 %all_to_all.38 = f32[8,24,128]{2,1,0:T(8,128)S(1)} all-to-all(f32[8,24,128]{2,1,0:T(8,128)S(1)} %broadcast_in_dim.4), channel_id=1, replica_groups=mesh['x'=4,'core'=2,'z'=8,'y'=4] {'z'}, dimensions={0} | all-to-all | bytes 196608 | tf_op jit(solution)/shard_map/all_to_all | solution.py:406
  253.0 0.8 broadcast_in_dim.5
  253.8 5.6 %all-to-all-start.6 = ((f32[32,24,128]{2,1,0:T(8,128)}), f32[32,24,128]{2,1,0:T(8,128)S(1)}, u32[]{:S(2)}, u32[]{:S(2)}) async-start(f32[32,24,128]{2,1,0:T(8,128)} %broadcast_in_dim.5), calls=%async_computation.6 | async-start | bytes 786432 | tf_op jit(solution)/shard_map/all_to_all | solution.py:406
  259.4 7.3 %shard_map.151 = bf16[1,12,384,128]{3,2,1,0:T(8,128)(2,1)} custom-call(bf16[32,96,384]{2,1,0:T(8,128)(2,1)} %all-to-all-done.3.d_ref.d_hbm, bf16[12,512,384]{2,1,0:T(8,128)(2,1)} %get-tuple-element.22.fac_ref.fac_hbm, bf16[6,256,384]{2,1,0:T(8,128)(2,1)} %get-tuple-element.26.dg_ref, bf16[512,128]{1,0:T(8,128)(2,1)} %get-tuple-element.27.w_ref, ...), custom_call_target="tpu_custom_call" | custom-call | flops 4000000000 | bytes 8421376 | tf_op jit(solution)/shard_map/pallas_call | solution.py:394
  266.7 2.8 %all-to-all-done.6 = f32[32,24,128]{2,1,0:T(8,128)S(1)} async-done(((f32[32,24,128]{2,1,0:T(8,128)}), f32[32,24,128]{2,1,0:T(8,128)S(1)}, u32[]{:S(2)}, u32[]{:S(2)}) %all-to-all-start.6) | async-done | bytes 393248 | tf_op jit(solution)/shard_map/all_to_all | solution.py:406
  269.5 0.7 slice_bitcast_fusion
  (3 shorter events, 0.1 us)
Async XLA Ops:
  78.6 32.6 %all-to-all-start.1 = ((bf16[32,48,384]{2,1,0:T(8,128)(2,1)}), bf16[32,48,384]{2,1,0:T(8,128)(2,1)S(1)}, u32[]{:S(2)}, u32[]{:S(2)}) async-start(bf16[32,48,384]{2,1,0:T(8,128)(2,1)} %get-tuple-element.18), calls=%async_computation.1 | async-start | bytes 2359296 | tf_op jit(solution)/shard_map/all_to_all | solution.py:406
  111.2 1.0 copy-start
  158.7 56.6 %all-to-all-start.3 = ((bf16[32,96,384]{2,1,0:T(8,128)(2,1)}), bf16[32,96,384]{2,1,0:T(8,128)(2,1)}, u32[]{:S(2)}, u32[]{:S(2)}) async-start(bf16[32,96,384]{2,1,0:T(8,128)(2,1)} %shard_map.148), calls=%async_computation.3 | async-start | bytes 4718592 | tf_op jit(solution)/shard_map/all_to_all | solution.py:406
  253.8 15.7 %all-to-all-start.6 = ((f32[32,24,128]{2,1,0:T(8,128)}), f32[32,24,128]{2,1,0:T(8,128)S(1)}, u32[]{:S(2)}, u32[]{:S(2)}) async-start(f32[32,24,128]{2,1,0:T(8,128)} %broadcast_in_dim.5), calls=%async_computation.6 | async-start | bytes 786432 | tf_op jit(solution)/shard_map/all_to_all | solution.py:406

commit v3 on v2

--- a/solution.py
+++ b/solution.py
@@ -310,10 +310,10 @@
     each(4, lambda c: kept(c).start())
     widen()
     for c in range(4):
-        de = take(wide_ref, c, total, 4)
+        de = take(wide_ref, c, total, 4).astype(BF16)
         kept(c).wait()
-        put(prod_ref, c, total, 8, dot(de.astype(BF16), lr_ref[2 * c + 1], 1, 0))
-        put(prod_ref, 4 + c, total, 8, dot(de.T.astype(BF16), lr_ref[2 * c], 1, 0))
+        put(prod_ref, c, total, 8, dot(de, lr_ref[2 * c + 1], 1, 0))
+        put(prod_ref, 4 + c, total, 8, dot(de, lr_ref[2 * c], 0, 0))
     for copy in narrowed(prod_ref, out_ref, out_hbm, out_sem):
         copy.wait()
 
@@ -334,7 +334,8 @@
 
 
 def weights_kernel(
-    z_hbm, d_hbm, fac_hbm, sums_hbm, out_ref, acc_ref, z_ref, d_ref, fac_ref, z_sem, d_sem, fac_sem, sums_sem
+    z_hbm, d_hbm, fac_hbm, sums_hbm, keep_ref, give_ref, out_ref, acc_ref, z_ref, d_ref, fac_ref,
+    z_sem, d_sem, fac_sem, sums_sem,
 ):
     rows, total, _ = z_ref.shape
 
@@ -352,8 +353,8 @@
     def step(m):
         for copy in came(m):
             copy.wait()
-        for h in range(2):
-            acc_ref[...] += dot(side_gradients(d_ref, fac_ref, m, h), z_ref[2 * m + h], 1, 0)
+        made = jnp.concatenate([side_gradients(d_ref, fac_ref, m, h) for h in range(2)], axis=1)
+        acc_ref[...] += dot(made, z_ref[two(m)].reshape(2 * total, C), 1, 0)
 
     each(rows // 2, begin)
     rest = pltpu.make_async_copy(sums_hbm, out_ref.at[pl.ds(4 * C, 2 * C)], sums_sem.at[0])
@@ -365,6 +366,10 @@
         out_ref[n * C : (n + 1) * C, :] = left.T
         out_ref[(2 + n) * C : (3 + n) * C, :] = right.T
     rest.wait()
+    half = 3 * C
+    keep = pl.multiple_of(lax.axis_index("core") * half, half)
+    keep_ref[...] = out_ref[pl.ds(keep, half), :]
+    give_ref[...] = out_ref[pl.ds(half - keep, half), :]
 
 
 def pair_kernel(d_ref, fac_ref, dg_ref, w_ref, wg_ref, out_ref, wt_ref):
@@ -382,7 +387,14 @@
     lax.fori_loop(0, rows // 2, body, 0)
 
 
-def call(body, outs, scratch, flops, *args, smem=(), hbm=(), hbm_out=(), sems=()):
+def call(body, outs, scratch, flops, *args, smem=(), hbm=(), hbm_out=(), sems=(), after=(), limit=62):
+    given = len(args)
+    args = (*args, *after)
+    hbm = (*hbm, *range(given, len(args)))
+
+    def inner(*refs):
+        body(*refs[:given], *refs[given + len(after) :])
+
     spaces = [pltpu.SMEM if n in smem else pltpu.HBM if n in hbm else pltpu.VMEM for n in range(len(args))]
     shapes = [jax.ShapeDtypeStruct(s, t) for s, t in outs]
     out_specs = [
@@ -392,18 +404,22 @@
         shapes, out_specs = shapes[0], out_specs[0]
     moved = sum(a.size * a.dtype.itemsize for a in args)
     return pl.pallas_call(
-        body,
+        inner,
         out_shape=shapes,
         in_specs=[pl.BlockSpec(memory_space=space) for space in spaces],
         out_specs=out_specs,
         scratch_shapes=[pltpu.VMEM(s, t) for s, t in scratch] + [pltpu.SemaphoreType.DMA((n,)) for n in sems],
-        compiler_params=pltpu.CompilerParams(vmem_limit_bytes=62 << 20),
+        compiler_params=pltpu.CompilerParams(vmem_limit_bytes=limit << 20),
         cost_estimate=pl.CostEstimate(flops=flops, bytes_accessed=moved, transcendentals=0),
     )(*args)
 
 
 def exchange(x, axis):
     return lax.all_to_all(x, axis, split_axis=0, concat_axis=0, tiled=True)
+
+
+def swap(x):
+    return lax.ppermute(x, "core", [(0, 1), (1, 0)])
 
 
 def on_device(
@@ -420,17 +436,17 @@
         [((4 * C, C), BF16), ((rows, total, C), BF16), ((4, C, C), BF16), ((32, 8 * rows, total), BF16)],
         4000 * mega, res_count, z, *sides, smem=(0,), hbm=(1, 2, 3, 4, 5), hbm_out=(0,), sems=(pairs, 4, pairs),
     )
-    blocks = exchange(blocks, DAP)
     factors, w_all = call(
         factors_kernel, [((rows, 4 * C, total), BF16), ((4 * C, C), BF16)], [], 4000 * mega,
-        res_count, z, *sides, smem=(0,),
+        res_count, z, *sides, smem=(0,), after=(blocks,),
     )
     scaled, factor, dnormed = call(
         gates_kernel,
         [((pairs, 2 * C, total), BF16), ((pairs, 2 * C, total), F32), ((pairs, 2 * C, total), F32)],
         [((C, C), BF16), ((2 * C, 2 * C), BF16)], 4000 * mega,
-        z, g, w_gate, w_out,
-    )
+        z, g, w_gate, w_out, after=(blocks,),
+    )
+    blocks = exchange(blocks, DAP)
     edges, lr = call(
         edges_kernel,
         [((32, 4 * rows, total), BF16), ((8, total, total), BF16)],
@@ -438,7 +454,7 @@
             ((total // C, 8 * total, C), F32), ((total // C, 4 * total, C), F32),
             ((8, total, total), BF16), ((32, 8 * rows, total), BF16), ((32, 4 * rows, total), BF16),
         ], 4000 * mega,
-        blocks, hbm=(0,), hbm_out=(0, 1), sems=(4, 4, 4),
+        blocks, hbm=(0,), hbm_out=(0, 1), sems=(4, 4, 4), after=(factors, dnormed),
     )
     edges = exchange(edges, DAP)
     dedges, normed = call(
@@ -451,12 +467,6 @@
         res_count, edges, dnormed, smem=(0,), hbm=(1, 2), hbm_out=(0, 1), sems=(rows // 4,) * 4,
     )
     dedges = exchange(dedges, DAP)
-    dgate, sums = call(
-        linear_kernel,
-        [((pairs, 2 * C, total), BF16), ((2 * C, C), F32)],
-        [((2 * C, 2 * C), BF16), ((C, C), F32), ((2 * C, 2 * C), F32)], 4000 * mega,
-        z, normed, scaled, factor, w_out,
-    )
     back = call(
         back_kernel,
         [((32, 8 * rows, total), BF16)],
@@ -466,27 +476,38 @@
         ], 4000 * mega,
         dedges, lr, hbm=(0, 1), hbm_out=(0,), sems=(4, 4, 4),
     )
+    dgate, sums = call(
+        linear_kernel,
+        [((pairs, 2 * C, total), BF16), ((2 * C, C), F32)],
+        [((2 * C, 2 * C), BF16), ((C, C), F32), ((2 * C, 2 * C), F32)], 4000 * mega,
+        z, normed, scaled, factor, w_out, after=(back,),
+    )
     back = exchange(back, DAP)
-    parts = call(
+    keep, give = call(
         weights_kernel,
-        [((6 * C, C), F32)],
+        [((3 * C, C), F32), ((3 * C, C), F32)],
         [
-            ((4 * C, C), F32), ((rows, total, C), BF16),
+            ((6 * C, C), F32), ((4 * C, C), F32), ((rows, total, C), BF16),
             ((32, 8 * rows, total), BF16), ((rows, 4 * C, total), BF16),
         ], 4000 * mega,
         z, back, factors, sums, hbm=(0, 1, 2, 3), sems=(pairs, pairs, pairs, 1),
     )
-    near = ("x", "core", "y")
-    share = exchange(parts.reshape(32, 24, C), near).sum(axis=0, keepdims=True)
+    share = exchange((keep + swap(give)).reshape(16, 24, C), ("x", "y")).sum(axis=0, keepdims=True)
     share = exchange(jnp.broadcast_to(share, (8, 24, C)), "z").sum(axis=0, keepdims=True)
-    whole = exchange(jnp.broadcast_to(share, (32, 24, C)), near).reshape(6, C, C)
+    share = jnp.broadcast_to(share, (16, 24, C))
     grad = call(
         pair_kernel,
         [((1, rows, total, C), BF16)],
         [((C, 4 * C), BF16)], 4000 * mega,
-        back, factors, dgate, w_all, w_gate,
-    )
-    return (grad, *(whole[n] for n in range(6)))
+        back, factors, dgate, w_all, w_gate, after=(share,),
+    )
+    mine, grad = lax.optimization_barrier((exchange(share, ("x", "y")), grad))
+    mine = mine.reshape(3, C, C)
+    other = swap(mine)
+    first = lax.axis_index("core") == 0
+    whole = [jnp.where(first, mine[n], other[n]) for n in range(3)]
+    whole += [jnp.where(first, other[n], mine[n]) for n in range(3)]
+    return (grad, *whole)
 
 
 def solution(mesh):

time: 271 us -> 269 us (level)
  blocking collectives: 138 us -> 95.4 us
  waiting for transfers between devices: 61.6 us -> 86.8 us
  starting transfers between devices: 15.3 us -> 30.8 us
    all_to_all x4, blocking collectives: 138 us -> 95.4 us  [exchange(): return lax.all_to_all(x, axis, split_axis=0, concat_axis=0, tiled=True)]
    all_to_all x3, waiting for transfers between devices: 61.6 us -> 84.5 us  [exchange(): return lax.all_to_all(x, axis, split_axis=0, concat_axis=0, tiled=True)]
    ppermute x0 -> x2, starting transfers between devices: none -> 9.3 us  [swap(): return lax.ppermute(x, 'core', [(0, 1), (1, 0)])]
    all_to_all x3, starting transfers between devices: 15.3 us -> 21.5 us  [exchange(): return lax.all_to_all(x, axis, split_axis=0, concat_axis=0, tiled=True)]
  transfers between devices with their start and end apart: 3 -> 5, of which waited for: 3 -> 4; matrix products, arithmetic and copies ran while one was open for 0% -> 0% of each run, Pallas kernels for 10% -> 10%
where the time goes in v3:
time: 269 us; the launch traced here: 268 us
  blocking collectives  95.4 us (35%)
  waiting for transfers between devices  86.8 us (32%)
  Pallas kernels  51.5 us (19%)
  starting transfers between devices  30.8 us (11%)
    all_to_all x4, blocking collectives, exchange(): return lax.all_to_all(x, axis, split_axis=0, concat_axis=0, tiled=True)  95.4 us
    all_to_all x3, waiting for transfers between devices, exchange(): return lax.all_to_all(x, axis, split_axis=0, concat_axis=0, tiled=True)  84.5 us
    pallas_call x9, Pallas kernels, call(): pl.pallas_call(inner, out_shape=shapes, in_specs=[pl.BlockSpec(memory_spa...  51.5 us
    all_to_all x3, starting transfers between devices, exchange(): return lax.all_to_all(x, axis, split_axis=0, concat_axis=0, tiled=True)  21.5 us
    ppermute x2, starting transfers between devices, swap(): return lax.ppermute(x, 'core', [(0, 1), (1, 0)])  9.3 us
  transfers between devices with their start and end apart: 5, of which 4 were waited for; matrix products, arithmetic and copies ran while one was open for 0% of the time, Pallas kernels for 10%

profile of v3, /device:TPU:1, one launch (start us, length us, event | category | flops | bytes accessed | tf_op | source)
XLA Modules:
  0.0 268.4 jit_solution(10134054731984879716)
XLA Ops:
  1.3 4.3 %shard_map.144.refs_6_.refs_4_ = bf16[32,96,384]{2,1,0:T(8,128)(2,1)} custom-call(s32[1]{0:T(128)S(6)} %copy.16.refs_0_, bf16[12,384,128]{2,1,0:T(8,128)(2,1)} %bitcast.20, bf16[128,128]{1,0:T(8,128)(2,1)} %refs_2_.4, bf16[128,128]{1,0:T(8,128)(2,1)} %refs_3_.4, bf16[128,128]{1,0:T(8,128)(2,1)} %refs_4_.5, bf16[128,128]{1,0:T(8,128)(2,1)} %refs_5_.3), custom_call_target="tpu_custom_call" | custom-call | flops 4000000000 | bytes 1310724 | tf_op jit(solution)/shard_map/pallas_call | solution.py:406
  5.6 12.1 %all-to-all-start = ((bf16[32,96,384]{2,1,0:T(8,128)(2,1)}), bf16[32,96,384]{2,1,0:T(8,128)(2,1)}, u32[]{:S(2)}, u32[]{:S(2)}) async-start(bf16[32,96,384]{2,1,0:T(8,128)(2,1)} %shard_map.144.refs_6_.refs_4_), calls=%async_computation | async-start | bytes 4718592 | tf_op jit(solution)/shard_map/all_to_all | solution.py:418
  17.8 7.5 %shard_map.145 = (bf16[12,512,384]{2,1,0:T(8,128)(2,1)}, bf16[512,128]{1,0:T(8,128)(2,1)}) custom-call(s32[1]{0:T(128)S(6)} %copy.16.refs_0_, bf16[12,384,128]{2,1,0:T(8,128)(2,1)} %bitcast.21, bf16[128,128]{1,0:T(8,128)(2,1)} %refs_2_.4, bf16[128,128]{1,0:T(8,128)(2,1)} %refs_3_.4, bf16[128,128]{1,0:T(8,128)(2,1)} %refs_4_.5, bf16[128,128]{1,0:T(8,128)(2,1)} %refs_5_.3, ...), custom_call_target="tpu_custom_call" | custom-call | flops 4000000000 | bytes 3670020 | tf_op jit(solution)/shard_map/pallas_call | solution.py:406
  25.3 6.9 %shard_map.146 = (bf16[6,256,384]{2,1,0:T(8,128)(2,1)}, f32[6,256,384]{2,1,0:T(8,128)}, f32[6,256,384]{2,1,0:T(8,128)}) custom-call(bf16[12,384,128]{2,1,0:T(8,128)(2,1)} %bitcast.22, bf16[12,384,128]{2,1,0:T(8,128)(2,1)} %bitcast.19, bf16[128,128]{1,0:T(8,128)(2,1)} %refs_4_.7, bf16[128,128]{1,0:T(8,128)(2,1)} %refs_4_.6, ...), custom_call_target="tpu_custom_call" | custom-call | flops 4000000000 | bytes 4784128 | tf_op jit(solution)/shard_map/pallas_call | solution.py:406
  32.2 39.4 %all-to-all-done.refs_0_ = bf16[32,96,384]{2,1,0:T(8,128)(2,1)} async-done(((bf16[32,96,384]{2,1,0:T(8,128)(2,1)}), bf16[32,96,384]{2,1,0:T(8,128)(2,1)}, u32[]{:S(2)}, u32[]{:S(2)}) %all-to-all-start) | async-done | bytes 2359328 | tf_op jit(solution)/shard_map/all_to_all | solution.py:418
  71.7 4.6 %shard_map.147 = (bf16[32,48,384]{2,1,0:T(8,128)(2,1)}, bf16[8,384,384]{2,1,0:T(8,128)(2,1)}) custom-call(bf16[32,96,384]{2,1,0:T(8,128)(2,1)} %all-to-all-done.refs_0_, bf16[12,512,384]{2,1,0:T(8,128)(2,1)} %get-tuple-element.22.refs_1_.refs_2_, f32[6,256,384]{2,1,0:T(8,128)} %get-tuple-element.23.refs_2_), custom_call_target="tpu_custom_call" | custom-call | flops 4000000000 | bytes 9437184 | tf_op jit(solution)/shard_map/pallas_call | solution.py:406
  76.3 37.7 %all_to_all.35.refs_1_ = bf16[32,48,384]{2,1,0:T(8,128)(2,1)} all-to-all(bf16[32,48,384]{2,1,0:T(8,128)(2,1)} %get-tuple-element.24), channel_id=1, replica_groups=mesh['x'=4,'core'=2,'z'=8,'y'=4] {'z','y'}, dimensions={0} | all-to-all | bytes 2359296 | tf_op jit(solution)/shard_map/all_to_all | solution.py:418
  114.0 3.8 %shard_map.148 = (bf16[32,48,384]{2,1,0:T(8,128)(2,1)}, bf16[6,256,384]{2,1,0:T(8,128)(2,1)}) custom-call(s32[1]{0:T(128)S(6)} %copy.16.refs_0_, bf16[32,48,384]{2,1,0:T(8,128)(2,1)} %all_to_all.35.refs_1_, f32[6,256,384]{2,1,0:T(8,128)} %get-tuple-element.23.refs_2_), custom_call_target="tpu_custom_call" | custom-call | flops 4000000000 | bytes 3538948 | tf_op jit(solution)/shard_map/pallas_call | solution.py:406
  117.8 33.8 %all_to_all.36.refs_0_ = bf16[32,48,384]{2,1,0:T(8,128)(2,1)} all-to-all(bf16[32,48,384]{2,1,0:T(8,128)(2,1)} %get-tuple-element.25), channel_id=1, replica_groups=mesh['x'=4,'core'=2,'z'=8,'y'=4] {'z','y'}, dimensions={0} | all-to-all | bytes 2359296 | tf_op jit(solution)/shard_map/all_to_all | solution.py:418
  151.7 5.8 %shard_map.149.refs_5_ = bf16[32,96,384]{2,1,0:T(8,128)(2,1)} custom-call(bf16[32,48,384]{2,1,0:T(8,128)(2,1)} %all_to_all.36.refs_0_, bf16[8,384,384]{2,1,0:T(8,128)(2,1)} %get-tuple-element.26.refs_1_), custom_call_target="tpu_custom_call" | custom-call | flops 4000000000 | bytes 3538944 | tf_op jit(solution)/shard_map/pallas_call | solution.py:406
  157.5 5.8 %all-to-all-start.3 = ((bf16[32,96,384]{2,1,0:T(8,128)(2,1)}), bf16[32,96,384]{2,1,0:T(8,128)(2,1)}, u32[]{:S(2)}, u32[]{:S(2)}) async-start(bf16[32,96,384]{2,1,0:T(8,128)(2,1)} %shard_map.149.refs_5_), calls=%async_computation.3 | async-start | bytes 4718592 | tf_op jit(solution)/shard_map/all_to_all | solution.py:418
  163.3 6.3 %shard_map.150 = (bf16[6,256,384]{2,1,0:T(8,128)(2,1)}, f32[256,128]{1,0:T(8,128)}) custom-call(bf16[12,384,128]{2,1,0:T(8,128)(2,1)} %bitcast.23, bf16[6,256,384]{2,1,0:T(8,128)(2,1)} %get-tuple-element.27.refs_1_, bf16[6,256,384]{2,1,0:T(8,128)(2,1)} %get-tuple-element.28.refs_2_, f32[6,256,384]{2,1,0:T(8,128)} %get-tuple-element.29.refs_3_, ...), custom_call_target="tpu_custom_call" | custom-call | flops 4000000000 | bytes 8290304 | tf_op jit(solution)/shard_map/pallas_call | solution.py:406
  169.7 45.0 %all-to-all-done.3.refs_1_.refs_0_ = bf16[32,96,384]{2,1,0:T(8,128)(2,1)} async-done(((bf16[32,96,384]{2,1,0:T(8,128)(2,1)}), bf16[32,96,384]{2,1,0:T(8,128)(2,1)}, u32[]{:S(2)}, u32[]{:S(2)}) %all-to-all-start.3) | async-done | bytes 2359328 | tf_op jit(solution)/shard_map/all_to_all | solution.py:418
  214.7 4.8 %shard_map.151 = (f32[384,128]{1,0:T(8,128)}, f32[384,128]{1,0:T(8,128)}) custom-call(bf16[12,384,128]{2,1,0:T(8,128)(2,1)} %bitcast.24, bf16[32,96,384]{2,1,0:T(8,128)(2,1)} %all-to-all-done.3.refs_1_.refs_0_, bf16[12,512,384]{2,1,0:T(8,128)(2,1)} %get-tuple-element.22.refs_1_.refs_2_, f32[256,128]{1,0:T(8,128)} %get-tuple-element.30.refs_3_), custom_call_target="tpu_custom_call" | custom-call | flops 4000000000 | bytes 8388608 | tf_op jit(solution)/shard_map/pallas_call | solution.py:406
  219.5 5.4 %collective-permute-start = (f32[384,128]{1,0:T(8,128)}, f32[384,128]{1,0:T(8,128)S(1)}, u32[]{:S(2)}, u32[]{:S(2)}) collective-permute-start(f32[384,128]{1,0:T(8,128)} %get-tuple-element.32), channel_id=1, source_target_pairs={{0,32},{32,0},{1,33},{33,1},{2,34},{34,2},{3,35},{35,3},{4,36},{36... | collective-permute-start | bytes 589832 | tf_op jit(solution)/shard_map/ppermute | solution.py:422
  224.9 1.3 collective-permute-done
  226.1 1.0 add.3
  227.1 13.5 %all_to_all.37 = f32[16,24,128]{2,1,0:T(8,128)S(1)} all-to-all(f32[16,24,128]{2,1,0:T(8,128)S(1)} %bitcast.18), channel_id=1, replica_groups=mesh['x'=4,'core'=2,'z'=8,'y'=4] {'x','y'}, dimensions={0} | all-to-all | bytes 393216 | tf_op jit(solution)/shard_map/all_to_all | solution.py:418
  240.7 10.4 %all_to_all.38 = f32[8,24,128]{2,1,0:T(8,128)S(1)} all-to-all(f32[8,24,128]{2,1,0:T(8,128)S(1)} %broadcast_in_dim.4), channel_id=1, replica_groups=mesh['x'=4,'core'=2,'z'=8,'y'=4] {'z'}, dimensions={0} | all-to-all | bytes 196608 | tf_op jit(solution)/shard_map/all_to_all | solution.py:418
  251.1 0.7 broadcast_in_dim.5.refs_5_
  251.8 3.5 %all-to-all-start.6 = ((f32[16,24,128]{2,1,0:T(8,128)}), f32[16,24,128]{2,1,0:T(8,128)S(1)}, u32[]{:S(2)}, u32[]{:S(2)}) async-start(f32[16,24,128]{2,1,0:T(8,128)} %broadcast_in_dim.5.refs_5_), calls=%async_computation.6 | async-start | bytes 393216 | tf_op jit(solution)/shard_map/all_to_all | solution.py:418
  255.3 7.3 %shard_map.152 = bf16[1,12,384,128]{3,2,1,0:T(8,128)(2,1)} custom-call(bf16[32,96,384]{2,1,0:T(8,128)(2,1)} %all-to-all-done.3.refs_1_.refs_0_, bf16[12,512,384]{2,1,0:T(8,128)(2,1)} %get-tuple-element.22.refs_1_.refs_2_, bf16[6,256,384]{2,1,0:T(8,128)(2,1)} %get-tuple-element.33.refs_2_, bf16[512,128]{1,0:T(8,128)(2,1)} %get-tuple-element.34.refs_3_, ...), custom_call_target="tpu_custom_call" | custom-call | flops 4000000000 | bytes 8617984 | tf_op jit(solution)/shard_map/pallas_call | solution.py:406
  262.6 0.0 all-to-all-done.6
  262.6 3.9 %collective-permute-start.1 = (f32[3,128,128]{2,1,0:T(8,128)S(1)}, f32[3,128,128]{2,1,0:T(8,128)S(1)}, u32[]{:S(2)}, u32[]{:S(2)}) collective-permute-start(f32[3,128,128]{2,1,0:T(8,128)S(1)} %bitcast.16), channel_id=1, source_target_pairs={{0,32},{32,0},{1,33},{33,1},{2,34},{34,2},{3,35},{35,3},{4,36},{36... | collective-permute-start | bytes 589832 | tf_op jit(solution)/shard_map/ppermute | solution.py:422
  266.5 1.1 collective-permute-done.1
  267.6 0.7 select_bitcast_fusion
  (3 shorter events, 0.0 us)
Async XLA Ops:
  5.6 66.1 %all-to-all-start = ((bf16[32,96,384]{2,1,0:T(8,128)(2,1)}), bf16[32,96,384]{2,1,0:T(8,128)(2,1)}, u32[]{:S(2)}, u32[]{:S(2)}) async-start(bf16[32,96,384]{2,1,0:T(8,128)(2,1)} %shard_map.144.refs_6_.refs_4_), calls=%async_computation | async-start | bytes 4718592 | tf_op jit(solution)/shard_map/all_to_all | solution.py:418
  157.5 57.2 %all-to-all-start.3 = ((bf16[32,96,384]{2,1,0:T(8,128)(2,1)}), bf16[32,96,384]{2,1,0:T(8,128)(2,1)}, u32[]{:S(2)}, u32[]{:S(2)}) async-start(bf16[32,96,384]{2,1,0:T(8,128)(2,1)} %shard_map.149.refs_5_), calls=%async_computation.3 | async-start | bytes 4718592 | tf_op jit(solution)/shard_map/all_to_all | solution.py:418
  219.5 6.6 %collective-permute-start = (f32[384,128]{1,0:T(8,128)}, f32[384,128]{1,0:T(8,128)S(1)}, u32[]{:S(2)}, u32[]{:S(2)}) collective-permute-start(f32[384,128]{1,0:T(8,128)} %get-tuple-element.32), channel_id=1, source_target_pairs={{0,32},{32,0},{1,33},{33,1},{2,34},{34,2},{3,35},{35,3},{4,36},{36... | collective-permute-start | bytes 589832 | tf_op jit(solution)/shard_map/ppermute | solution.py:422
  251.8 10.9 %all-to-all-start.6 = ((f32[16,24,128]{2,1,0:T(8,128)}), f32[16,24,128]{2,1,0:T(8,128)S(1)}, u32[]{:S(2)}, u32[]{:S(2)}) async-start(f32[16,24,128]{2,1,0:T(8,128)} %broadcast_in_dim.5.refs_5_), calls=%async_computation.6 | async-start | bytes 393216 | tf_op jit(solution)/shard_map/all_to_all | solution.py:418
  262.6 5.0 %collective-permute-start.1 = (f32[3,128,128]{2,1,0:T(8,128)S(1)}, f32[3,128,128]{2,1,0:T(8,128)S(1)}, u32[]{:S(2)}, u32[]{:S(2)}) collective-permute-start(f32[3,128,128]{2,1,0:T(8,128)S(1)} %bitcast.16), channel_id=1, source_target_pairs={{0,32},{32,0},{1,33},{33,1},{2,34},{34,2},{3,35},{35,3},{4,36},{36... | collective-permute-start | bytes 589832 | tf_op jit(solution)/shard_map/ppermute | solution.py:422

commit v4 on v3

--- a/solution.py
+++ b/solution.py
@@ -161,25 +161,27 @@
     return lambda: each(4, lambda n: copy(n).start()), lambda: each(4, step)
 
 
-def edges_kernel(x_hbm, out_hbm, lr_hbm, wide_ref, prod_ref, lr_ref, x_ref, out_ref, lr_sem, x_sem, out_sem):
+def edges_kernel(x_hbm, out_hbm, wide_ref, prod_ref, x_ref, out_ref, x_sem, out_sem):
     total = x_ref.shape[2]
     fetch, widen = widen_all(x_hbm, x_ref, wide_ref, x_sem)
     fetch()
     widen()
-
-    def kept(c):
-        return pltpu.make_async_copy(lr_ref.at[two(c)], lr_hbm.at[two(c)], lr_sem.at[c])
-
     for c in range(4):
         left = take(wide_ref, c, total, 8).astype(BF16)
         right = take(wide_ref, 4 + c, total, 8).astype(BF16)
-        lr_ref[2 * c] = left
-        lr_ref[2 * c + 1] = right
-        kept(c).start()
         put(prod_ref, c, total, 4, dot(left, right, 1, 1))
     for copy in narrowed(prod_ref, out_ref, out_hbm, out_sem):
         copy.wait()
-    each(4, lambda c: kept(c).wait())
+
+
+def split_kernel(x_hbm, out_ref, wide_ref, x_ref, x_sem):
+    total = x_ref.shape[2]
+    fetch, widen = widen_all(x_hbm, x_ref, wide_ref, x_sem)
+    fetch()
+    widen()
+    for c in range(4):
+        out_ref[2 * c] = take(wide_ref, c, total, 8).astype(BF16)
+        out_ref[2 * c + 1] = take(wide_ref, 4 + c, total, 8).astype(BF16)
 
 
 def narrowed(prod_ref, out_ref, out_hbm, sem):
@@ -200,7 +202,7 @@
     return copies
 
 
-def gates_kernel(z_ref, g_ref, wg_ref, wo_ref, ds_ref, fac_ref, dn_ref, wgt_ref, wx_ref):
+def gates_kernel(z_ref, g_ref, wg_ref, wo_ref, ds_ref, fac_ref, wx_ref, dn_ref, wgt_ref):
     rows = z_ref.shape[0]
     wgt_ref[...] = wg_ref[...].astype(F32).T.astype(BF16)
     wx_ref[...] = spread_rows(wo_ref[...])
@@ -226,9 +228,17 @@
     return jnp.where(top, first, second) * (1.0 / C)
 
 
-def norm_kernel(
-    count_ref, e_hbm, dn_hbm, de_hbm, nm_hbm, e_ref, dn_ref, de_ref, nm_ref, e_sem, dn_sem, de_sem, nm_sem
-):
+def standard(e):
+    shifted = e - chan_mean(e)[None]
+    rs = lax.rsqrt(chan_mean(shifted * shifted) + 1e-05)
+    return shifted * rs[None], rs
+
+
+def cell_mask(count, row, total):
+    return row_mask(count, row + iota((8, total), 0) // 4, (8, total))
+
+
+def norm_kernel(count_ref, e_hbm, dn_hbm, de_hbm, e_ref, dn_ref, de_ref, e_sem, dn_sem, de_sem):
     devices, block, total = e_ref.shape
     rows = block // 4
     count = count_ref[0]
@@ -241,18 +251,11 @@
         )
 
     def gone(q):
-        return (
-            pltpu.make_async_copy(de_ref.at[:, tile(q)], de_hbm.at[:, tile(q)], de_sem.at[q]),
-            pltpu.make_async_copy(nm_ref.at[two(q)], nm_hbm.at[two(q)], nm_sem.at[q]),
-        )
+        return pltpu.make_async_copy(de_ref.at[:, tile(q)], de_hbm.at[:, tile(q)], de_sem.at[q])
 
     def begin(q):
         for copy in came(q):
             copy.start()
-
-    def finish(q):
-        for copy in gone(q):
-            copy.wait()
 
     def step(q):
         for copy in came(q):
@@ -260,29 +263,34 @@
         e_all = e_ref[:, tile(q), :].astype(F32)
         halves = []
         for h in range(2):
-            e = e_all[:, 8 * h : 8 * h + 8, :]
-            row = start + 4 * q + 2 * h + iota((8, total), 0) // 4
-            mask = row_mask(count, row, (8, total))
-            shifted = e - chan_mean(e)[None]
-            rs = lax.rsqrt(chan_mean(shifted * shifted) + 1e-05)
-            xhat = shifted * rs[None]
-            nm_ref[2 * q + h] = (xhat * mask[None]).reshape(2 * C, total).astype(BF16)
+            xhat, rs = standard(e_all[:, 8 * h : 8 * h + 8, :])
+            mask = cell_mask(count, start + 4 * q + 2 * h, total)
             dn = dn_ref[2 * q + h].reshape(32, 8, total)
             m1 = chan_mean(dn)
             m2 = chan_mean(dn * xhat)
             halves.append((mask * rs)[None] * (dn - m1[None] - xhat * m2[None]))
         de_ref[:, tile(q), :] = jnp.concatenate(halves, axis=1).astype(BF16)
-        for copy in gone(q):
-            copy.start()
+        gone(q).start()
 
     each(rows // 4, begin)
     each(rows // 4, step)
-    each(rows // 4, finish)
-
-
-def linear_kernel(z_ref, nm_ref, ds_ref, fac_ref, wo_ref, dg_ref, sums_ref, wx_ref, ga_ref, oa_ref):
-    rows = z_ref.shape[0]
-    wx_ref[...] = spread_rows(wo_ref[...]).astype(F32).T.astype(BF16)
+    each(rows // 4, lambda q: gone(q).wait())
+
+
+def linear_kernel(count_ref, z_ref, e_ref, ds_ref, fac_ref, wx_in_ref, dg_ref, sums_ref, wx_ref, nm_ref, ga_ref, oa_ref):
+    rows, total, _ = z_ref.shape
+    count = count_ref[0]
+    start = first_row(rows)
+
+    def normalize(q):
+        e_all = e_ref[:, tile(q), :].astype(F32)
+        for h in range(2):
+            xhat, _ = standard(e_all[:, 8 * h : 8 * h + 8, :])
+            mask = cell_mask(count, start + 4 * q + 2 * h, total)
+            nm_ref[2 * q + h] = (xhat * mask[None]).reshape(2 * C, total).astype(BF16)
+
+    each(rows // 4, normalize)
+    wx_ref[...] = wx_in_ref[...].astype(F32).T.astype(BF16)
     ga_ref[...] = jnp.zeros_like(ga_ref)
     oa_ref[...] = jnp.zeros_like(oa_ref)
 
@@ -440,31 +448,36 @@
         factors_kernel, [((rows, 4 * C, total), BF16), ((4 * C, C), BF16)], [], 4000 * mega,
         res_count, z, *sides, smem=(0,), after=(blocks,),
     )
-    scaled, factor, dnormed = call(
+    scaled, factor, spread, dnormed = call(
         gates_kernel,
-        [((pairs, 2 * C, total), BF16), ((pairs, 2 * C, total), F32), ((pairs, 2 * C, total), F32)],
-        [((C, C), BF16), ((2 * C, 2 * C), BF16)], 4000 * mega,
+        [((pairs, 2 * C, total), BF16), ((pairs, 2 * C, total), F32), ((2 * C, 2 * C), BF16),
+         ((pairs, 2 * C, total), F32)],
+        [((C, C), BF16)], 4000 * mega,
         z, g, w_gate, w_out, after=(blocks,),
     )
     blocks = exchange(blocks, DAP)
-    edges, lr = call(
+    edges = call(
         edges_kernel,
-        [((32, 4 * rows, total), BF16), ((8, total, total), BF16)],
+        [((32, 4 * rows, total), BF16)],
         [
             ((total // C, 8 * total, C), F32), ((total // C, 4 * total, C), F32),
-            ((8, total, total), BF16), ((32, 8 * rows, total), BF16), ((32, 4 * rows, total), BF16),
+            ((32, 8 * rows, total), BF16), ((32, 4 * rows, total), BF16),
         ], 4000 * mega,
-        blocks, hbm=(0,), hbm_out=(0, 1), sems=(4, 4, 4), after=(factors, dnormed),
+        blocks, hbm=(0,), hbm_out=(0,), sems=(4, 4), after=(factors, scaled),
     )
     edges = exchange(edges, DAP)
-    dedges, normed = call(
+    dedges = call(
         norm_kernel,
-        [((32, 4 * rows, total), BF16), ((pairs, 2 * C, total), BF16)],
+        [((32, 4 * rows, total), BF16)],
         [
-            ((32, 4 * rows, total), BF16), ((pairs, 2 * C, total), F32),
-            ((32, 4 * rows, total), BF16), ((pairs, 2 * C, total), BF16),
+            ((32, 4 * rows, total), BF16), ((pairs, 2 * C, total), F32), ((32, 4 * rows, total), BF16),
         ], 4000 * mega,
-        res_count, edges, dnormed, smem=(0,), hbm=(1, 2), hbm_out=(0, 1), sems=(rows // 4,) * 4,
+        res_count, edges, dnormed, smem=(0,), hbm=(1, 2), hbm_out=(0,), sems=(rows // 4,) * 3,
+    )
+    lr = call(
+        split_kernel, [((8, total, total), BF16)],
+        [((total // C, 8 * total, C), F32), ((32, 8 * rows, total), BF16)], 4000 * mega,
+        blocks, hbm=(0,), sems=(4,), after=(dedges,),
     )
     dedges = exchange(dedges, DAP)
     back = call(
@@ -474,13 +487,13 @@
             ((total // C, 4 * total, C), F32), ((total // C, 8 * total, C), F32),
             ((8, total, total), BF16), ((32, 4 * rows, total), BF16), ((32, 8 * rows, total), BF16),
         ], 4000 * mega,
-        dedges, lr, hbm=(0, 1), hbm_out=(0,), sems=(4, 4, 4),
+        dedges, lr, hbm=(0, 1), hbm_out=(0,), sems=(4, 4, 4), limit=52,
     )
     dgate, sums = call(
         linear_kernel,
         [((pairs, 2 * C, total), BF16), ((2 * C, C), F32)],
-        [((2 * C, 2 * C), BF16), ((C, C), F32), ((2 * C, 2 * C), F32)], 4000 * mega,
-        z, normed, scaled, factor, w_out, after=(back,),
+        [((2 * C, 2 * C), BF16), ((pairs, 2 * C, total), BF16), ((C, C), F32), ((2 * C, 2 * C), F32)], 4000 * mega,
+        res_count, z, edges, scaled, factor, spread, smem=(0,), after=(back,),
     )
     back = exchange(back, DAP)
     keep, give = call(

time: 269 us -> 268 us (level)
  blocking collectives: 95.4 us -> 61.6 us
  waiting for transfers between devices: 86.8 us -> 109 us
  starting transfers between devices: 30.8 us -> 37.2 us
  Pallas kernels: 51.5 us -> 55.7 us
    all_to_all x4 -> x3, blocking collectives: 95.4 us -> 61.6 us  [exchange(): return lax.all_to_all(x, axis, split_axis=0, concat_axis=0, tiled=True)]
    all_to_all x3 -> x4, waiting for transfers between devices: 84.5 us -> 107 us  [exchange(): return lax.all_to_all(x, axis, split_axis=0, concat_axis=0, tiled=True)]
    all_to_all x3 -> x4, starting transfers between devices: 21.5 us -> 27.8 us  [exchange(): return lax.all_to_all(x, axis, split_axis=0, concat_axis=0, tiled=True)]
    pallas_call x9 -> x10, Pallas kernels: 51.5 us -> 55.7 us  [call(): pl.pallas_call(inner, out_shape=shapes, in_specs=[pl.BlockSpec(memory_spa...]
  transfers between devices with their start and end apart: 5 -> 6, of which waited for: 4 -> 5; matrix products, arithmetic and copies ran while one was open for 0% -> 0% of each run, Pallas kernels for 10% -> 12%
where the time goes in v4:
time: 268 us; the launch traced here: 267 us
  waiting for transfers between devices  109 us (41%)
  blocking collectives  61.6 us (23%)
  Pallas kernels  55.7 us (21%)
  starting transfers between devices  37.2 us (14%)
    all_to_all x4, waiting for transfers between devices, exchange(): return lax.all_to_all(x, axis, split_axis=0, concat_axis=0, tiled=True)  107 us
    all_to_all x3, blocking collectives, exchange(): return lax.all_to_all(x, axis, split_axis=0, concat_axis=0, tiled=True)  61.6 us
    pallas_call x10, Pallas kernels, call(): pl.pallas_call(inner, out_shape=shapes, in_specs=[pl.BlockSpec(memory_spa...  55.7 us
    all_to_all x4, starting transfers between devices, exchange(): return lax.all_to_all(x, axis, split_axis=0, concat_axis=0, tiled=True)  27.8 us
    ppermute x2, starting transfers between devices, swap(): return lax.ppermute(x, 'core', [(0, 1), (1, 0)])  9.47 us
  transfers between devices with their start and end apart: 6, of which 5 were waited for; matrix products, arithmetic and copies ran while one was open for 0% of the time, Pallas kernels for 12%

profile of v4, /device:TPU:1, one launch (start us, length us, event | category | flops | bytes accessed | tf_op | source)
XLA Modules:
  0.0 267.5 jit_solution(1048546447828122192)
XLA Ops:
  1.3 4.3 %shard_map.144.refs_6_.refs_4_ = bf16[32,96,384]{2,1,0:T(8,128)(2,1)} custom-call(s32[1]{0:T(128)S(6)} %copy.16.refs_0_, bf16[12,384,128]{2,1,0:T(8,128)(2,1)} %bitcast.20, bf16[128,128]{1,0:T(8,128)(2,1)} %refs_2_.4, bf16[128,128]{1,0:T(8,128)(2,1)} %refs_3_.4, bf16[128,128]{1,0:T(8,128)(2,1)} %refs_4_.4, bf16[128,128]{1,0:T(8,128)(2,1)} %refs_5_.3), custom_call_target="tpu_custom_call" | custom-call | flops 4000000000 | bytes 1310724 | tf_op jit(solution)/shard_map/pallas_call | solution.py:414
  5.6 12.1 %all-to-all-start = ((bf16[32,96,384]{2,1,0:T(8,128)(2,1)}), bf16[32,96,384]{2,1,0:T(8,128)(2,1)}, u32[]{:S(2)}, u32[]{:S(2)}) async-start(bf16[32,96,384]{2,1,0:T(8,128)(2,1)} %shard_map.144.refs_6_.refs_4_), calls=%async_computation | async-start | bytes 4718592 | tf_op jit(solution)/shard_map/all_to_all | solution.py:426
  17.8 7.5 %shard_map.145 = (bf16[12,512,384]{2,1,0:T(8,128)(2,1)}, bf16[512,128]{1,0:T(8,128)(2,1)}) custom-call(s32[1]{0:T(128)S(6)} %copy.16.refs_0_, bf16[12,384,128]{2,1,0:T(8,128)(2,1)} %bitcast.21, bf16[128,128]{1,0:T(8,128)(2,1)} %refs_2_.4, bf16[128,128]{1,0:T(8,128)(2,1)} %refs_3_.4, bf16[128,128]{1,0:T(8,128)(2,1)} %refs_4_.4, bf16[128,128]{1,0:T(8,128)(2,1)} %refs_5_.3, ...), custom_call_target="tpu_custom_call" | custom-call | flops 4000000000 | bytes 3670020 | tf_op jit(solution)/shard_map/pallas_call | solution.py:414
  25.3 7.0 %shard_map.146 = (bf16[6,256,384]{2,1,0:T(8,128)(2,1)}, f32[6,256,384]{2,1,0:T(8,128)}, bf16[256,256]{1,0:T(8,128)(2,1)}, f32[6,256,384]{2,1,0:T(8,128)}) custom-call(bf16[12,384,128]{2,1,0:T(8,128)(2,1)} %bitcast.22, bf16[12,384,128]{2,1,0:T(8,128)(2,1)} %bitcast.19, bf16[128,128]{1,0:T(8,128)(2,1)} %refs_4_.5, bf16[128,128]{1,0:T(8,128)(2,1)} %refs_3_.5, ...), custom_call_target="tpu_custom_call" | custom-call | flops 4000000000 | bytes 4784128 | tf_op jit(solution)/shard_map/pallas_call | solution.py:414
  32.3 39.4 %all-to-all-done.refs_0_ = bf16[32,96,384]{2,1,0:T(8,128)(2,1)} async-done(((bf16[32,96,384]{2,1,0:T(8,128)(2,1)}), bf16[32,96,384]{2,1,0:T(8,128)(2,1)}, u32[]{:S(2)}, u32[]{:S(2)}) %all-to-all-start) | async-done | bytes 2359328 | tf_op jit(solution)/shard_map/all_to_all | solution.py:426
  71.7 4.0 %shard_map.147 = bf16[32,48,384]{2,1,0:T(8,128)(2,1)} custom-call(bf16[32,96,384]{2,1,0:T(8,128)(2,1)} %all-to-all-done.refs_0_, bf16[12,512,384]{2,1,0:T(8,128)(2,1)} %get-tuple-element.19.refs_1_.refs_2_, bf16[6,256,384]{2,1,0:T(8,128)(2,1)} %get-tuple-element.20.refs_2_.refs_3_), custom_call_target="tpu_custom_call" | custom-call | flops 4000000000 | bytes 8257536 | tf_op jit(solution)/shard_map/pallas_call | solution.py:414
  75.6 37.6 %all_to_all.35.refs_1_.refs_2_ = bf16[32,48,384]{2,1,0:T(8,128)(2,1)} all-to-all(bf16[32,48,384]{2,1,0:T(8,128)(2,1)} %shard_map.147), channel_id=1, replica_groups=mesh['x'=4,'core'=2,'z'=8,'y'=4] {'z','y'}, dimensions={0} | all-to-all | bytes 2359296 | tf_op jit(solution)/shard_map/all_to_all | solution.py:426
  113.2 3.6 %shard_map.148.refs_1_ = bf16[32,48,384]{2,1,0:T(8,128)(2,1)} custom-call(s32[1]{0:T(128)S(6)} %copy.16.refs_0_, bf16[32,48,384]{2,1,0:T(8,128)(2,1)} %all_to_all.35.refs_1_.refs_2_, f32[6,256,384]{2,1,0:T(8,128)} %get-tuple-element.21.refs_2_), custom_call_target="tpu_custom_call" | custom-call | flops 4000000000 | bytes 3538948 | tf_op jit(solution)/shard_map/pallas_call | solution.py:414
  116.8 5.0 %all-to-all-start.2 = ((bf16[32,48,384]{2,1,0:T(8,128)(2,1)}), bf16[32,48,384]{2,1,0:T(8,128)(2,1)S(1)}, u32[]{:S(2)}, u32[]{:S(2)}) async-start(bf16[32,48,384]{2,1,0:T(8,128)(2,1)} %shard_map.148.refs_1_), calls=%async_computation.2 | async-start | bytes 2359296 | tf_op jit(solution)/shard_map/all_to_all | solution.py:426
  121.8 4.4 %shard_map.149.refs_1_ = bf16[8,384,384]{2,1,0:T(8,128)(2,1)} custom-call(bf16[32,96,384]{2,1,0:T(8,128)(2,1)} %all-to-all-done.refs_0_, bf16[32,48,384]{2,1,0:T(8,128)(2,1)} %shard_map.148.refs_1_), custom_call_target="tpu_custom_call" | custom-call | flops 4000000000 | bytes 3538944 | tf_op jit(solution)/shard_map/pallas_call | solution.py:414
  126.2 23.4 %all-to-all-done.2.refs_0_ = bf16[32,48,384]{2,1,0:T(8,128)(2,1)S(1)} async-done(((bf16[32,48,384]{2,1,0:T(8,128)(2,1)}), bf16[32,48,384]{2,1,0:T(8,128)(2,1)S(1)}, u32[]{:S(2)}, u32[]{:S(2)}) %all-to-all-start.2) | async-done | bytes 1179680 | tf_op jit(solution)/shard_map/all_to_all | solution.py:426
  149.6 5.7 %shard_map.150.refs_6_ = bf16[32,96,384]{2,1,0:T(8,128)(2,1)} custom-call(bf16[32,48,384]{2,1,0:T(8,128)(2,1)S(1)} %all-to-all-done.2.refs_0_, bf16[8,384,384]{2,1,0:T(8,128)(2,1)} %shard_map.149.refs_1_), custom_call_target="tpu_custom_call" | custom-call | flops 4000000000 | bytes 3538944 | tf_op jit(solution)/shard_map/pallas_call | solution.py:414
  155.3 7.1 %all-to-all-start.3 = ((bf16[32,96,384]{2,1,0:T(8,128)(2,1)}), bf16[32,96,384]{2,1,0:T(8,128)(2,1)}, u32[]{:S(2)}, u32[]{:S(2)}) async-start(bf16[32,96,384]{2,1,0:T(8,128)(2,1)} %shard_map.150.refs_6_), calls=%async_computation.3 | async-start | bytes 4718592 | tf_op jit(solution)/shard_map/all_to_all | solution.py:426
  162.4 7.1 %shard_map.151 = (bf16[6,256,384]{2,1,0:T(8,128)(2,1)}, f32[256,128]{1,0:T(8,128)}) custom-call(s32[1]{0:T(128)S(6)} %copy.16.refs_0_, bf16[12,384,128]{2,1,0:T(8,128)(2,1)} %bitcast.23, bf16[32,48,384]{2,1,0:T(8,128)(2,1)} %all_to_all.35.refs_1_.refs_2_, bf16[6,256,384]{2,1,0:T(8,128)(2,1)} %get-tuple-element.20.refs_2_.refs_3_, ...), custom_call_target="tpu_custom_call" | custom-call | flops 4000000000 | bytes 8388612 | tf_op jit(solution)/shard_map/pallas_call | solution.py:414
  169.5 44.1 %all-to-all-done.3.refs_1_.refs_0_ = bf16[32,96,384]{2,1,0:T(8,128)(2,1)} async-done(((bf16[32,96,384]{2,1,0:T(8,128)(2,1)}), bf16[32,96,384]{2,1,0:T(8,128)(2,1)}, u32[]{:S(2)}, u32[]{:S(2)}) %all-to-all-start.3) | async-done | bytes 2359328 | tf_op jit(solution)/shard_map/all_to_all | solution.py:426
  213.5 4.8 %shard_map.152 = (f32[384,128]{1,0:T(8,128)}, f32[384,128]{1,0:T(8,128)}) custom-call(bf16[12,384,128]{2,1,0:T(8,128)(2,1)} %bitcast.24, bf16[32,96,384]{2,1,0:T(8,128)(2,1)} %all-to-all-done.3.refs_1_.refs_0_, bf16[12,512,384]{2,1,0:T(8,128)(2,1)} %get-tuple-element.19.refs_1_.refs_2_, f32[256,128]{1,0:T(8,128)} %get-tuple-element.24.refs_3_), custom_call_target="tpu_custom_call" | custom-call | flops 4000000000 | bytes 8388608 | tf_op jit(solution)/shard_map/pallas_call | solution.py:414
  218.4 5.5 %collective-permute-start = (f32[384,128]{1,0:T(8,128)}, f32[384,128]{1,0:T(8,128)S(1)}, u32[]{:S(2)}, u32[]{:S(2)}) collective-permute-start(f32[384,128]{1,0:T(8,128)} %get-tuple-element.26), channel_id=1, source_target_pairs={{0,32},{32,0},{1,33},{33,1},{2,34},{34,2},{3,35},{35,3},{4,36},{36... | collective-permute-start | bytes 589832 | tf_op jit(solution)/shard_map/ppermute | solution.py:430
  223.9 1.3 collective-permute-done
  225.2 1.0 add.3
  226.1 13.6 %all_to_all.36 = f32[16,24,128]{2,1,0:T(8,128)S(1)} all-to-all(f32[16,24,128]{2,1,0:T(8,128)S(1)} %bitcast.18), channel_id=1, replica_groups=mesh['x'=4,'core'=2,'z'=8,'y'=4] {'x','y'}, dimensions={0} | all-to-all | bytes 393216 | tf_op jit(solution)/shard_map/all_to_all | solution.py:426
  239.8 10.4 %all_to_all.37 = f32[8,24,128]{2,1,0:T(8,128)S(1)} all-to-all(f32[8,24,128]{2,1,0:T(8,128)S(1)} %broadcast_in_dim.4), channel_id=1, replica_groups=mesh['x'=4,'core'=2,'z'=8,'y'=4] {'z'}, dimensions={0} | all-to-all | bytes 196608 | tf_op jit(solution)/shard_map/all_to_all | solution.py:426
  250.2 0.7 broadcast_in_dim.5.refs_5_
  250.9 3.5 %all-to-all-start.6 = ((f32[16,24,128]{2,1,0:T(8,128)}), f32[16,24,128]{2,1,0:T(8,128)S(1)}, u32[]{:S(2)}, u32[]{:S(2)}) async-start(f32[16,24,128]{2,1,0:T(8,128)} %broadcast_in_dim.5.refs_5_), calls=%async_computation.6 | async-start | bytes 393216 | tf_op jit(solution)/shard_map/all_to_all | solution.py:426
  254.4 7.3 %shard_map.153 = bf16[1,12,384,128]{3,2,1,0:T(8,128)(2,1)} custom-call(bf16[32,96,384]{2,1,0:T(8,128)(2,1)} %all-to-all-done.3.refs_1_.refs_0_, bf16[12,512,384]{2,1,0:T(8,128)(2,1)} %get-tuple-element.19.refs_1_.refs_2_, bf16[6,256,384]{2,1,0:T(8,128)(2,1)} %get-tuple-element.27.refs_2_, bf16[512,128]{1,0:T(8,128)(2,1)} %get-tuple-element.28.refs_3_, ...), custom_call_target="tpu_custom_call" | custom-call | flops 4000000000 | bytes 8617984 | tf_op jit(solution)/shard_map/pallas_call | solution.py:414
  261.7 0.0 all-to-all-done.6
  261.7 3.9 %collective-permute-start.1 = (f32[3,128,128]{2,1,0:T(8,128)S(1)}, f32[3,128,128]{2,1,0:T(8,128)S(1)}, u32[]{:S(2)}, u32[]{:S(2)}) collective-permute-start(f32[3,128,128]{2,1,0:T(8,128)S(1)} %bitcast.16), channel_id=1, source_target_pairs={{0,32},{32,0},{1,33},{33,1},{2,34},{34,2},{3,35},{35,3},{4,36},{36... | collective-permute-start | bytes 589832 | tf_op jit(solution)/shard_map/ppermute | solution.py:430
  265.7 1.1 collective-permute-done.1
  266.7 0.7 select_bitcast_fusion
  (3 shorter events, 0.0 us)
Async XLA Ops:
  5.6 66.1 %all-to-all-start = ((bf16[32,96,384]{2,1,0:T(8,128)(2,1)}), bf16[32,96,384]{2,1,0:T(8,128)(2,1)}, u32[]{:S(2)}, u32[]{:S(2)}) async-start(bf16[32,96,384]{2,1,0:T(8,128)(2,1)} %shard_map.144.refs_6_.refs_4_), calls=%async_computation | async-start | bytes 4718592 | tf_op jit(solution)/shard_map/all_to_all | solution.py:426
  116.8 32.7 %all-to-all-start.2 = ((bf16[32,48,384]{2,1,0:T(8,128)(2,1)}), bf16[32,48,384]{2,1,0:T(8,128)(2,1)S(1)}, u32[]{:S(2)}, u32[]{:S(2)}) async-start(bf16[32,48,384]{2,1,0:T(8,128)(2,1)} %shard_map.148.refs_1_), calls=%async_computation.2 | async-start | bytes 2359296 | tf_op jit(solution)/shard_map/all_to_all | solution.py:426
  155.3 58.2 %all-to-all-start.3 = ((bf16[32,96,384]{2,1,0:T(8,128)(2,1)}), bf16[32,96,384]{2,1,0:T(8,128)(2,1)}, u32[]{:S(2)}, u32[]{:S(2)}) async-start(bf16[32,96,384]{2,1,0:T(8,128)(2,1)} %shard_map.150.refs_6_), calls=%async_computation.3 | async-start | bytes 4718592 | tf_op jit(solution)/shard_map/all_to_all | solution.py:426
  218.4 6.8 %collective-permute-start = (f32[384,128]{1,0:T(8,128)}, f32[384,128]{1,0:T(8,128)S(1)}, u32[]{:S(2)}, u32[]{:S(2)}) collective-permute-start(f32[384,128]{1,0:T(8,128)} %get-tuple-element.26), channel_id=1, source_target_pairs={{0,32},{32,0},{1,33},{33,1},{2,34},{34,2},{3,35},{35,3},{4,36},{36... | collective-permute-start | bytes 589832 | tf_op jit(solution)/shard_map/ppermute | solution.py:430
  250.9 10.8 %all-to-all-start.6 = ((f32[16,24,128]{2,1,0:T(8,128)}), f32[16,24,128]{2,1,0:T(8,128)S(1)}, u32[]{:S(2)}, u32[]{:S(2)}) async-start(f32[16,24,128]{2,1,0:T(8,128)} %broadcast_in_dim.5.refs_5_), calls=%async_computation.6 | async-start | bytes 393216 | tf_op jit(solution)/shard_map/all_to_all | solution.py:426
  261.7 5.0 %collective-permute-start.1 = (f32[3,128,128]{2,1,0:T(8,128)S(1)}, f32[3,128,128]{2,1,0:T(8,128)S(1)}, u32[]{:S(2)}, u32[]{:S(2)}) collective-permute-start(f32[3,128,128]{2,1,0:T(8,128)S(1)} %bitcast.16), channel_id=1, source_target_pairs={{0,32},{32,0},{1,33},{33,1},{2,34},{34,2},{3,35},{35,3},{4,36},{36... | collective-permute-start | bytes 589832 | tf_op jit(solution)/shard_map/ppermute | solution.py:430

commit v5 on v4

--- a/solution.py
+++ b/solution.py
@@ -503,7 +503,7 @@
             ((6 * C, C), F32), ((4 * C, C), F32), ((rows, total, C), BF16),
             ((32, 8 * rows, total), BF16), ((rows, 4 * C, total), BF16),
         ], 4000 * mega,
-        z, back, factors, sums, hbm=(0, 1, 2, 3), sems=(pairs, pairs, pairs, 1),
+        z, back, factors, sums, hbm=(0, 1, 2, 3), sems=(pairs, pairs, pairs, 1), limit=50,
     )
     share = exchange((keep + swap(give)).reshape(16, 24, C), ("x", "y")).sum(axis=0, keepdims=True)
     share = exchange(jnp.broadcast_to(share, (8, 24, C)), "z").sum(axis=0, keepdims=True)
@@ -512,7 +512,7 @@
         pair_kernel,
         [((1, rows, total, C), BF16)],
         [((C, 4 * C), BF16)], 4000 * mega,
-        back, factors, dgate, w_all, w_gate, after=(share,),
+        back, factors, dgate, w_all, w_gate, after=(share,), limit=50,
     )
     mine, grad = lax.optimization_barrier((exchange(share, ("x", "y")), grad))
     mine = mine.reshape(3, C, C)

time: 268 us -> 268 us (level)
  no operation moved by 1% of the time
where the time goes in v5:
time: 268 us; the launch traced here: 267 us
  waiting for transfers between devices  109 us (41%)
  blocking collectives  61.6 us (23%)
  Pallas kernels  55 us (21%)
  starting transfers between devices  37.5 us (14%)
    all_to_all x4, waiting for transfers between devices, exchange(): return lax.all_to_all(x, axis, split_axis=0, concat_axis=0, tiled=True)  107 us
    all_to_all x3, blocking collectives, exchange(): return lax.all_to_all(x, axis, split_axis=0, concat_axis=0, tiled=True)  61.6 us
    pallas_call x10, Pallas kernels, call(): pl.pallas_call(inner, out_shape=shapes, in_specs=[pl.BlockSpec(memory_spa...  55 us
    all_to_all x4, starting transfers between devices, exchange(): return lax.all_to_all(x, axis, split_axis=0, concat_axis=0, tiled=True)  27.7 us
    ppermute x2, starting transfers between devices, swap(): return lax.ppermute(x, 'core', [(0, 1), (1, 0)])  9.85 us
  transfers between devices with their start and end apart: 6, of which 5 were waited for; matrix products, arithmetic and copies ran while one was open for 0% of the time, Pallas kernels for 12%

profile of v5, /device:TPU:1, one launch (start us, length us, event | category | flops | bytes accessed | tf_op | source)
XLA Modules:
  0.0 266.9 jit_solution(8981533320442874566)
XLA Ops:
  1.3 4.3 %shard_map.144.refs_6_.refs_4_ = bf16[32,96,384]{2,1,0:T(8,128)(2,1)} custom-call(s32[1]{0:T(128)S(6)} %copy.16.refs_0_, bf16[12,384,128]{2,1,0:T(8,128)(2,1)} %bitcast.16, bf16[128,128]{1,0:T(8,128)(2,1)} %refs_2_.4, bf16[128,128]{1,0:T(8,128)(2,1)} %refs_3_.4, bf16[128,128]{1,0:T(8,128)(2,1)} %refs_4_.4, bf16[128,128]{1,0:T(8,128)(2,1)} %refs_5_.3), custom_call_target="tpu_custom_call" | custom-call | flops 4000000000 | bytes 1310724 | tf_op jit(solution)/shard_map/pallas_call | solution.py:414
  5.6 12.1 %all-to-all-start = ((bf16[32,96,384]{2,1,0:T(8,128)(2,1)}), bf16[32,96,384]{2,1,0:T(8,128)(2,1)}, u32[]{:S(2)}, u32[]{:S(2)}) async-start(bf16[32,96,384]{2,1,0:T(8,128)(2,1)} %shard_map.144.refs_6_.refs_4_), calls=%async_computation | async-start | bytes 4718592 | tf_op jit(solution)/shard_map/all_to_all | solution.py:426
  17.8 7.5 %shard_map.145 = (bf16[12,512,384]{2,1,0:T(8,128)(2,1)}, bf16[512,128]{1,0:T(8,128)(2,1)}) custom-call(s32[1]{0:T(128)S(6)} %copy.16.refs_0_, bf16[12,384,128]{2,1,0:T(8,128)(2,1)} %bitcast.17, bf16[128,128]{1,0:T(8,128)(2,1)} %refs_2_.4, bf16[128,128]{1,0:T(8,128)(2,1)} %refs_3_.4, bf16[128,128]{1,0:T(8,128)(2,1)} %refs_4_.4, bf16[128,128]{1,0:T(8,128)(2,1)} %refs_5_.3, ...), custom_call_target="tpu_custom_call" | custom-call | flops 4000000000 | bytes 3670020 | tf_op jit(solution)/shard_map/pallas_call | solution.py:414
  25.3 7.0 %shard_map.146 = (bf16[6,256,384]{2,1,0:T(8,128)(2,1)}, f32[6,256,384]{2,1,0:T(8,128)}, bf16[256,256]{1,0:T(8,128)(2,1)}, f32[6,256,384]{2,1,0:T(8,128)}) custom-call(bf16[12,384,128]{2,1,0:T(8,128)(2,1)} %bitcast.18, bf16[12,384,128]{2,1,0:T(8,128)(2,1)} %bitcast.24, bf16[128,128]{1,0:T(8,128)(2,1)} %refs_4_.5, bf16[128,128]{1,0:T(8,128)(2,1)} %refs_3_.5, ...), custom_call_target="tpu_custom_call" | custom-call | flops 4000000000 | bytes 4784128 | tf_op jit(solution)/shard_map/pallas_call | solution.py:414
  32.3 39.4 %all-to-all-done.refs_0_ = bf16[32,96,384]{2,1,0:T(8,128)(2,1)} async-done(((bf16[32,96,384]{2,1,0:T(8,128)(2,1)}), bf16[32,96,384]{2,1,0:T(8,128)(2,1)}, u32[]{:S(2)}, u32[]{:S(2)}) %all-to-all-start) | async-done | bytes 2359328 | tf_op jit(solution)/shard_map/all_to_all | solution.py:426
  71.7 4.0 %shard_map.147 = bf16[32,48,384]{2,1,0:T(8,128)(2,1)} custom-call(bf16[32,96,384]{2,1,0:T(8,128)(2,1)} %all-to-all-done.refs_0_, bf16[12,512,384]{2,1,0:T(8,128)(2,1)} %get-tuple-element.19.refs_1_.refs_2_, bf16[6,256,384]{2,1,0:T(8,128)(2,1)} %get-tuple-element.20.refs_2_.refs_3_), custom_call_target="tpu_custom_call" | custom-call | flops 4000000000 | bytes 8257536 | tf_op jit(solution)/shard_map/pallas_call | solution.py:414
  75.6 37.7 %all_to_all.35.refs_1_.refs_2_ = bf16[32,48,384]{2,1,0:T(8,128)(2,1)} all-to-all(bf16[32,48,384]{2,1,0:T(8,128)(2,1)} %shard_map.147), channel_id=1, replica_groups=mesh['x'=4,'core'=2,'z'=8,'y'=4] {'z','y'}, dimensions={0} | all-to-all | bytes 2359296 | tf_op jit(solution)/shard_map/all_to_all | solution.py:426
  113.3 3.6 %shard_map.148.refs_1_ = bf16[32,48,384]{2,1,0:T(8,128)(2,1)} custom-call(s32[1]{0:T(128)S(6)} %copy.16.refs_0_, bf16[32,48,384]{2,1,0:T(8,128)(2,1)} %all_to_all.35.refs_1_.refs_2_, f32[6,256,384]{2,1,0:T(8,128)} %get-tuple-element.21.refs_2_), custom_call_target="tpu_custom_call" | custom-call | flops 4000000000 | bytes 3538948 | tf_op jit(solution)/shard_map/pallas_call | solution.py:414
  116.9 4.9 %all-to-all-start.2 = ((bf16[32,48,384]{2,1,0:T(8,128)(2,1)}), bf16[32,48,384]{2,1,0:T(8,128)(2,1)S(1)}, u32[]{:S(2)}, u32[]{:S(2)}) async-start(bf16[32,48,384]{2,1,0:T(8,128)(2,1)} %shard_map.148.refs_1_), calls=%async_computation.2 | async-start | bytes 2359296 | tf_op jit(solution)/shard_map/all_to_all | solution.py:426
  121.8 4.4 %shard_map.149.refs_1_ = bf16[8,384,384]{2,1,0:T(8,128)(2,1)} custom-call(bf16[32,96,384]{2,1,0:T(8,128)(2,1)} %all-to-all-done.refs_0_, bf16[32,48,384]{2,1,0:T(8,128)(2,1)} %shard_map.148.refs_1_), custom_call_target="tpu_custom_call" | custom-call | flops 4000000000 | bytes 3538944 | tf_op jit(solution)/shard_map/pallas_call | solution.py:414
  126.2 23.4 %all-to-all-done.2.refs_0_ = bf16[32,48,384]{2,1,0:T(8,128)(2,1)S(1)} async-done(((bf16[32,48,384]{2,1,0:T(8,128)(2,1)}), bf16[32,48,384]{2,1,0:T(8,128)(2,1)S(1)}, u32[]{:S(2)}, u32[]{:S(2)}) %all-to-all-start.2) | async-done | bytes 1179680 | tf_op jit(solution)/shard_map/all_to_all | solution.py:426
  149.6 5.7 %shard_map.150.refs_6_ = bf16[32,96,384]{2,1,0:T(8,128)(2,1)} custom-call(bf16[32,48,384]{2,1,0:T(8,128)(2,1)S(1)} %all-to-all-done.2.refs_0_, bf16[8,384,384]{2,1,0:T(8,128)(2,1)} %shard_map.149.refs_1_), custom_call_target="tpu_custom_call" | custom-call | flops 4000000000 | bytes 3538944 | tf_op jit(solution)/shard_map/pallas_call | solution.py:414
  155.3 7.1 %all-to-all-start.3 = ((bf16[32,96,384]{2,1,0:T(8,128)(2,1)}), bf16[32,96,384]{2,1,0:T(8,128)(2,1)}, u32[]{:S(2)}, u32[]{:S(2)}) async-start(bf16[32,96,384]{2,1,0:T(8,128)(2,1)} %shard_map.150.refs_6_), calls=%async_computation.3 | async-start | bytes 4718592 | tf_op jit(solution)/shard_map/all_to_all | solution.py:426
  162.4 0.0 copy-start
  162.4 7.2 %shard_map.151 = (bf16[6,256,384]{2,1,0:T(8,128)(2,1)}, f32[256,128]{1,0:T(8,128)}) custom-call(s32[1]{0:T(128)S(6)} %copy.16.refs_0_, bf16[12,384,128]{2,1,0:T(8,128)(2,1)} %bitcast.19, bf16[32,48,384]{2,1,0:T(8,128)(2,1)} %all_to_all.35.refs_1_.refs_2_, bf16[6,256,384]{2,1,0:T(8,128)(2,1)} %get-tuple-element.20.refs_2_.refs_3_, ...), custom_call_target="tpu_custom_call" | custom-call | flops 4000000000 | bytes 8388612 | tf_op jit(solution)/shard_map/pallas_call | solution.py:414
  169.6 43.9 %all-to-all-done.3.refs_1_.refs_0_ = bf16[32,96,384]{2,1,0:T(8,128)(2,1)} async-done(((bf16[32,96,384]{2,1,0:T(8,128)(2,1)}), bf16[32,96,384]{2,1,0:T(8,128)(2,1)}, u32[]{:S(2)}, u32[]{:S(2)}) %all-to-all-start.3) | async-done | bytes 2359328 | tf_op jit(solution)/shard_map/all_to_all | solution.py:426
  213.5 0.0 copy-done
  213.6 0.9 copy-done.4
  214.5 4.5 %shard_map.152 = (f32[384,128]{1,0:T(8,128)S(1)}, f32[384,128]{1,0:T(8,128)S(1)}) custom-call(bf16[12,384,128]{2,1,0:T(8,128)(2,1)S(1)} %bitcast.20, bf16[32,96,384]{2,1,0:T(8,128)(2,1)} %all-to-all-done.3.refs_1_.refs_0_, bf16[12,512,384]{2,1,0:T(8,128)(2,1)} %get-tuple-element.19.refs_1_.refs_2_, f32[256,128]{1,0:T(8,128)S(1)} %copy-done.4), custom_call_target="tpu_custom_call" | custom-call | flops 4000000000 | bytes 8388608 | tf_op jit(solution)/shard_map/pallas_call | solution.py:414
  218.9 0.0 copy-start.1
  219.0 5.6 %collective-permute-start = (f32[384,128]{1,0:T(8,128)S(1)}, f32[384,128]{1,0:T(8,128)S(1)}, u32[]{:S(2)}, u32[]{:S(2)}) collective-permute-start(f32[384,128]{1,0:T(8,128)S(1)} %get-tuple-element.26), channel_id=1, source_target_pairs={{0,32},{32,0},{1,33},{33,1},{2,34},{34,2},{3,35},{35,3},{4,36},{36... | collective-permute-start | bytes 589832 | tf_op jit(solution)/shard_map/ppermute | solution.py:430
  224.5 1.1 collective-permute-done
  225.6 13.6 %all_to_all.36 = f32[16,24,128]{2,1,0:T(8,128)S(1)} all-to-all(f32[16,24,128]{2,1,0:T(8,128)S(1)} %bitcast.23), channel_id=1, replica_groups=mesh['x'=4,'core'=2,'z'=8,'y'=4] {'x','y'}, dimensions={0} | all-to-all | bytes 393216 | tf_op jit(solution)/shard_map/all_to_all | solution.py:426
  239.2 10.4 %all_to_all.37 = f32[8,24,128]{2,1,0:T(8,128)S(1)} all-to-all(f32[8,24,128]{2,1,0:T(8,128)S(1)} %broadcast_in_dim.4), channel_id=1, replica_groups=mesh['x'=4,'core'=2,'z'=8,'y'=4] {'z'}, dimensions={0} | all-to-all | bytes 196608 | tf_op jit(solution)/shard_map/all_to_all | solution.py:426
  249.6 0.7 broadcast_in_dim.5.refs_5_
  250.3 3.5 %all-to-all-start.6 = ((f32[16,24,128]{2,1,0:T(8,128)}), f32[16,24,128]{2,1,0:T(8,128)S(1)}, u32[]{:S(2)}, u32[]{:S(2)}) async-start(f32[16,24,128]{2,1,0:T(8,128)} %broadcast_in_dim.5.refs_5_), calls=%async_computation.6 | async-start | bytes 393216 | tf_op jit(solution)/shard_map/all_to_all | solution.py:426
  253.9 0.0 copy-done.1
  253.9 6.9 %shard_map.153 = bf16[1,12,384,128]{3,2,1,0:T(8,128)(2,1)} custom-call(bf16[32,96,384]{2,1,0:T(8,128)(2,1)} %all-to-all-done.3.refs_1_.refs_0_, bf16[12,512,384]{2,1,0:T(8,128)(2,1)} %get-tuple-element.19.refs_1_.refs_2_, bf16[6,256,384]{2,1,0:T(8,128)(2,1)S(1)} %copy-done.2, bf16[512,128]{1,0:T(8,128)(2,1)S(1)} %copy-done.3, ...), custom_call_target="tpu_custom_call" | custom-call | flops 4000000000 | bytes 8617984 | tf_op jit(solution)/shard_map/pallas_call | solution.py:414
  260.8 0.0 all-to-all-done.6
  260.8 4.3 %collective-permute-start.1 = (f32[3,128,128]{2,1,0:T(8,128)S(1)}, f32[3,128,128]{2,1,0:T(8,128)S(1)}, u32[]{:S(2)}, u32[]{:S(2)}) collective-permute-start(f32[3,128,128]{2,1,0:T(8,128)S(1)} %bitcast.21), channel_id=1, source_target_pairs={{0,32},{32,0},{1,33},{33,1},{2,34},{34,2},{3,35},{35,3},{4,36},{36... | collective-permute-start | bytes 589832 | tf_op jit(solution)/shard_map/ppermute | solution.py:430
  265.1 1.1 collective-permute-done.1
  266.2 0.7 select_bitcast_fusion
  (9 shorter events, 0.1 us)
Async XLA Ops:
  5.6 66.1 %all-to-all-start = ((bf16[32,96,384]{2,1,0:T(8,128)(2,1)}), bf16[32,96,384]{2,1,0:T(8,128)(2,1)}, u32[]{:S(2)}, u32[]{:S(2)}) async-start(bf16[32,96,384]{2,1,0:T(8,128)(2,1)} %shard_map.144.refs_6_.refs_4_), calls=%async_computation | async-start | bytes 4718592 | tf_op jit(solution)/shard_map/all_to_all | solution.py:426
  116.9 32.7 %all-to-all-start.2 = ((bf16[32,48,384]{2,1,0:T(8,128)(2,1)}), bf16[32,48,384]{2,1,0:T(8,128)(2,1)S(1)}, u32[]{:S(2)}, u32[]{:S(2)}) async-start(bf16[32,48,384]{2,1,0:T(8,128)(2,1)} %shard_map.148.refs_1_), calls=%async_computation.2 | async-start | bytes 2359296 | tf_op jit(solution)/shard_map/all_to_all | solution.py:426
  155.3 58.2 %all-to-all-start.3 = ((bf16[32,96,384]{2,1,0:T(8,128)(2,1)}), bf16[32,96,384]{2,1,0:T(8,128)(2,1)}, u32[]{:S(2)}, u32[]{:S(2)}) async-start(bf16[32,96,384]{2,1,0:T(8,128)(2,1)} %shard_map.150.refs_6_), calls=%async_computation.3 | async-start | bytes 4718592 | tf_op jit(solution)/shard_map/all_to_all | solution.py:426
  162.4 51.2 %copy-start = (bf16[1,12,384,128]{3,2,1,0:T(8,128)(2,1)S(1)}, bf16[1,12,384,128]{3,2,1,0:T(8,128)(2,1)}, u32[]{:S(2)}) copy-start(bf16[1,12,384,128]{3,2,1,0:T(8,128)(2,1)} %param.9) | copy-start | bytes 3538948
  213.5 0.9 copy-start.4
  218.9 34.9 %copy-start.1 = (bf16[128,128]{1,0:T(8,128)(2,1)S(1)}, bf16[128,128]{1,0:T(8,128)(2,1)}, u32[]{:S(2)}) copy-start(bf16[128,128]{1,0:T(8,128)(2,1)} %refs_4_.5) | copy-start | bytes 98308
  219.0 34.9 %copy-start.2 = (bf16[6,256,384]{2,1,0:T(8,128)(2,1)S(1)}, bf16[6,256,384]{2,1,0:T(8,128)(2,1)}, u32[]{:S(2)}) copy-start(bf16[6,256,384]{2,1,0:T(8,128)(2,1)} %get-tuple-element.27.refs_2_) | copy-start | bytes 3538948
  219.0 34.9 %copy-start.3 = (bf16[512,128]{1,0:T(8,128)(2,1)S(1)}, bf16[512,128]{1,0:T(8,128)(2,1)}, u32[]{:S(2)}) copy-start(bf16[512,128]{1,0:T(8,128)(2,1)} %get-tuple-element.28.refs_3_) | copy-start | bytes 393220
  219.0 6.6 %collective-permute-start = (f32[384,128]{1,0:T(8,128)S(1)}, f32[384,128]{1,0:T(8,128)S(1)}, u32[]{:S(2)}, u32[]{:S(2)}) collective-permute-start(f32[384,128]{1,0:T(8,128)S(1)} %get-tuple-element.26), channel_id=1, source_target_pairs={{0,32},{32,0},{1,33},{33,1},{2,34},{34,2},{3,35},{35,3},{4,36},{36... | collective-permute-start | bytes 589832 | tf_op jit(solution)/shard_map/ppermute | solution.py:430
  250.3 10.5 %all-to-all-start.6 = ((f32[16,24,128]{2,1,0:T(8,128)}), f32[16,24,128]{2,1,0:T(8,128)S(1)}, u32[]{:S(2)}, u32[]{:S(2)}) async-start(f32[16,24,128]{2,1,0:T(8,128)} %broadcast_in_dim.5.refs_5_), calls=%async_computation.6 | async-start | bytes 393216 | tf_op jit(solution)/shard_map/all_to_all | solution.py:426
  260.8 5.4 %collective-permute-start.1 = (f32[3,128,128]{2,1,0:T(8,128)S(1)}, f32[3,128,128]{2,1,0:T(8,128)S(1)}, u32[]{:S(2)}, u32[]{:S(2)}) collective-permute-start(f32[3,128,128]{2,1,0:T(8,128)S(1)} %bitcast.21), channel_id=1, source_target_pairs={{0,32},{32,0},{1,33},{33,1},{2,34},{34,2},{3,35},{35,3},{4,36},{36... | collective-permute-start | bytes 589832 | tf_op jit(solution)/shard_map/ppermute | solution.py:430

commit v6 on v5

--- a/solution.py
+++ b/solution.py
@@ -503,7 +503,7 @@
             ((6 * C, C), F32), ((4 * C, C), F32), ((rows, total, C), BF16),
             ((32, 8 * rows, total), BF16), ((rows, 4 * C, total), BF16),
         ], 4000 * mega,
-        z, back, factors, sums, hbm=(0, 1, 2, 3), sems=(pairs, pairs, pairs, 1), limit=50,
+        z, back, factors, sums, hbm=(0, 1, 2, 3), sems=(pairs, pairs, pairs, 1), limit=52,
     )
     share = exchange((keep + swap(give)).reshape(16, 24, C), ("x", "y")).sum(axis=0, keepdims=True)
     share = exchange(jnp.broadcast_to(share, (8, 24, C)), "z").sum(axis=0, keepdims=True)

time: 268 us -> 268 us (level)
  no operation moved by 1% of the time
where the time goes in v6:
time: 268 us; the launch traced here: 267 us
  waiting for transfers between devices  109 us (41%)
  blocking collectives  61.6 us (23%)
  Pallas kernels  55 us (21%)
  starting transfers between devices  37.5 us (14%)
    all_to_all x4, waiting for transfers between devices, exchange(): return lax.all_to_all(x, axis, split_axis=0, concat_axis=0, tiled=True)  107 us
    all_to_all x3, blocking collectives, exchange(): return lax.all_to_all(x, axis, split_axis=0, concat_axis=0, tiled=True)  61.6 us
    pallas_call x10, Pallas kernels, call(): pl.pallas_call(inner, out_shape=shapes, in_specs=[pl.BlockSpec(memory_spa...  55 us
    all_to_all x4, starting transfers between devices, exchange(): return lax.all_to_all(x, axis, split_axis=0, concat_axis=0, tiled=True)  27.7 us
    ppermute x2, starting transfers between devices, swap(): return lax.ppermute(x, 'core', [(0, 1), (1, 0)])  9.85 us
  transfers between devices with their start and end apart: 6, of which 5 were waited for; matrix products, arithmetic and copies ran while one was open for 0% of the time, Pallas kernels for 12%

profile of v6, /device:TPU:1, one launch (start us, length us, event | category | flops | bytes accessed | tf_op | source)
XLA Modules:
  0.0 266.9 jit_solution(16599428265118097388)
XLA Ops:
  1.3 4.3 %shard_map.144.refs_6_.refs_4_ = bf16[32,96,384]{2,1,0:T(8,128)(2,1)} custom-call(s32[1]{0:T(128)S(6)} %copy.16.refs_0_, bf16[12,384,128]{2,1,0:T(8,128)(2,1)} %bitcast.16, bf16[128,128]{1,0:T(8,128)(2,1)} %refs_2_.4, bf16[128,128]{1,0:T(8,128)(2,1)} %refs_3_.4, bf16[128,128]{1,0:T(8,128)(2,1)} %refs_4_.4, bf16[128,128]{1,0:T(8,128)(2,1)} %refs_5_.3), custom_call_target="tpu_custom_call" | custom-call | flops 4000000000 | bytes 1310724 | tf_op jit(solution)/shard_map/pallas_call | solution.py:414
  5.6 12.1 %all-to-all-start = ((bf16[32,96,384]{2,1,0:T(8,128)(2,1)}), bf16[32,96,384]{2,1,0:T(8,128)(2,1)}, u32[]{:S(2)}, u32[]{:S(2)}) async-start(bf16[32,96,384]{2,1,0:T(8,128)(2,1)} %shard_map.144.refs_6_.refs_4_), calls=%async_computation | async-start | bytes 4718592 | tf_op jit(solution)/shard_map/all_to_all | solution.py:426
  17.8 7.5 %shard_map.145 = (bf16[12,512,384]{2,1,0:T(8,128)(2,1)}, bf16[512,128]{1,0:T(8,128)(2,1)}) custom-call(s32[1]{0:T(128)S(6)} %copy.16.refs_0_, bf16[12,384,128]{2,1,0:T(8,128)(2,1)} %bitcast.17, bf16[128,128]{1,0:T(8,128)(2,1)} %refs_2_.4, bf16[128,128]{1,0:T(8,128)(2,1)} %refs_3_.4, bf16[128,128]{1,0:T(8,128)(2,1)} %refs_4_.4, bf16[128,128]{1,0:T(8,128)(2,1)} %refs_5_.3, ...), custom_call_target="tpu_custom_call" | custom-call | flops 4000000000 | bytes 3670020 | tf_op jit(solution)/shard_map/pallas_call | solution.py:414
  25.3 7.0 %shard_map.146 = (bf16[6,256,384]{2,1,0:T(8,128)(2,1)}, f32[6,256,384]{2,1,0:T(8,128)}, bf16[256,256]{1,0:T(8,128)(2,1)}, f32[6,256,384]{2,1,0:T(8,128)}) custom-call(bf16[12,384,128]{2,1,0:T(8,128)(2,1)} %bitcast.18, bf16[12,384,128]{2,1,0:T(8,128)(2,1)} %bitcast.24, bf16[128,128]{1,0:T(8,128)(2,1)} %refs_4_.5, bf16[128,128]{1,0:T(8,128)(2,1)} %refs_3_.5, ...), custom_call_target="tpu_custom_call" | custom-call | flops 4000000000 | bytes 4784128 | tf_op jit(solution)/shard_map/pallas_call | solution.py:414
  32.3 39.4 %all-to-all-done.refs_0_ = bf16[32,96,384]{2,1,0:T(8,128)(2,1)} async-done(((bf16[32,96,384]{2,1,0:T(8,128)(2,1)}), bf16[32,96,384]{2,1,0:T(8,128)(2,1)}, u32[]{:S(2)}, u32[]{:S(2)}) %all-to-all-start) | async-done | bytes 2359328 | tf_op jit(solution)/shard_map/all_to_all | solution.py:426
  71.7 4.0 %shard_map.147 = bf16[32,48,384]{2,1,0:T(8,128)(2,1)} custom-call(bf16[32,96,384]{2,1,0:T(8,128)(2,1)} %all-to-all-done.refs_0_, bf16[12,512,384]{2,1,0:T(8,128)(2,1)} %get-tuple-element.19.refs_1_.refs_2_, bf16[6,256,384]{2,1,0:T(8,128)(2,1)} %get-tuple-element.20.refs_2_.refs_3_), custom_call_target="tpu_custom_call" | custom-call | flops 4000000000 | bytes 8257536 | tf_op jit(solution)/shard_map/pallas_call | solution.py:414
  75.6 37.7 %all_to_all.35.refs_1_.refs_2_ = bf16[32,48,384]{2,1,0:T(8,128)(2,1)} all-to-all(bf16[32,48,384]{2,1,0:T(8,128)(2,1)} %shard_map.147), channel_id=1, replica_groups=mesh['x'=4,'core'=2,'z'=8,'y'=4] {'z','y'}, dimensions={0} | all-to-all | bytes 2359296 | tf_op jit(solution)/shard_map/all_to_all | solution.py:426
  113.3 3.6 %shard_map.148.refs_1_ = bf16[32,48,384]{2,1,0:T(8,128)(2,1)} custom-call(s32[1]{0:T(128)S(6)} %copy.16.refs_0_, bf16[32,48,384]{2,1,0:T(8,128)(2,1)} %all_to_all.35.refs_1_.refs_2_, f32[6,256,384]{2,1,0:T(8,128)} %get-tuple-element.21.refs_2_), custom_call_target="tpu_custom_call" | custom-call | flops 4000000000 | bytes 3538948 | tf_op jit(solution)/shard_map/pallas_call | solution.py:414
  116.9 4.9 %all-to-all-start.2 = ((bf16[32,48,384]{2,1,0:T(8,128)(2,1)}), bf16[32,48,384]{2,1,0:T(8,128)(2,1)S(1)}, u32[]{:S(2)}, u32[]{:S(2)}) async-start(bf16[32,48,384]{2,1,0:T(8,128)(2,1)} %shard_map.148.refs_1_), calls=%async_computation.2 | async-start | bytes 2359296 | tf_op jit(solution)/shard_map/all_to_all | solution.py:426
  121.8 4.4 %shard_map.149.refs_1_ = bf16[8,384,384]{2,1,0:T(8,128)(2,1)} custom-call(bf16[32,96,384]{2,1,0:T(8,128)(2,1)} %all-to-all-done.refs_0_, bf16[32,48,384]{2,1,0:T(8,128)(2,1)} %shard_map.148.refs_1_), custom_call_target="tpu_custom_call" | custom-call | flops 4000000000 | bytes 3538944 | tf_op jit(solution)/shard_map/pallas_call | solution.py:414
  126.2 23.4 %all-to-all-done.2.refs_0_ = bf16[32,48,384]{2,1,0:T(8,128)(2,1)S(1)} async-done(((bf16[32,48,384]{2,1,0:T(8,128)(2,1)}), bf16[32,48,384]{2,1,0:T(8,128)(2,1)S(1)}, u32[]{:S(2)}, u32[]{:S(2)}) %all-to-all-start.2) | async-done | bytes 1179680 | tf_op jit(solution)/shard_map/all_to_all | solution.py:426
  149.6 5.7 %shard_map.150.refs_6_ = bf16[32,96,384]{2,1,0:T(8,128)(2,1)} custom-call(bf16[32,48,384]{2,1,0:T(8,128)(2,1)S(1)} %all-to-all-done.2.refs_0_, bf16[8,384,384]{2,1,0:T(8,128)(2,1)} %shard_map.149.refs_1_), custom_call_target="tpu_custom_call" | custom-call | flops 4000000000 | bytes 3538944 | tf_op jit(solution)/shard_map/pallas_call | solution.py:414
  155.3 7.1 %all-to-all-start.3 = ((bf16[32,96,384]{2,1,0:T(8,128)(2,1)}), bf16[32,96,384]{2,1,0:T(8,128)(2,1)}, u32[]{:S(2)}, u32[]{:S(2)}) async-start(bf16[32,96,384]{2,1,0:T(8,128)(2,1)} %shard_map.150.refs_6_), calls=%async_computation.3 | async-start | bytes 4718592 | tf_op jit(solution)/shard_map/all_to_all | solution.py:426
  162.4 0.0 copy-start
  162.4 7.2 %shard_map.151 = (bf16[6,256,384]{2,1,0:T(8,128)(2,1)}, f32[256,128]{1,0:T(8,128)}) custom-call(s32[1]{0:T(128)S(6)} %copy.16.refs_0_, bf16[12,384,128]{2,1,0:T(8,128)(2,1)} %bitcast.19, bf16[32,48,384]{2,1,0:T(8,128)(2,1)} %all_to_all.35.refs_1_.refs_2_, bf16[6,256,384]{2,1,0:T(8,128)(2,1)} %get-tuple-element.20.refs_2_.refs_3_, ...), custom_call_target="tpu_custom_call" | custom-call | flops 4000000000 | bytes 8388612 | tf_op jit(solution)/shard_map/pallas_call | solution.py:414
  169.6 43.9 %all-to-all-done.3.refs_1_.refs_0_ = bf16[32,96,384]{2,1,0:T(8,128)(2,1)} async-done(((bf16[32,96,384]{2,1,0:T(8,128)(2,1)}), bf16[32,96,384]{2,1,0:T(8,128)(2,1)}, u32[]{:S(2)}, u32[]{:S(2)}) %all-to-all-start.3) | async-done | bytes 2359328 | tf_op jit(solution)/shard_map/all_to_all | solution.py:426
  213.5 0.0 copy-done
  213.6 0.9 copy-done.4
  214.5 4.5 %shard_map.152 = (f32[384,128]{1,0:T(8,128)S(1)}, f32[384,128]{1,0:T(8,128)S(1)}) custom-call(bf16[12,384,128]{2,1,0:T(8,128)(2,1)S(1)} %bitcast.20, bf16[32,96,384]{2,1,0:T(8,128)(2,1)} %all-to-all-done.3.refs_1_.refs_0_, bf16[12,512,384]{2,1,0:T(8,128)(2,1)} %get-tuple-element.19.refs_1_.refs_2_, f32[256,128]{1,0:T(8,128)S(1)} %copy-done.4), custom_call_target="tpu_custom_call" | custom-call | flops 4000000000 | bytes 8388608 | tf_op jit(solution)/shard_map/pallas_call | solution.py:414
  218.9 0.0 copy-start.1
  219.0 5.6 %collective-permute-start = (f32[384,128]{1,0:T(8,128)S(1)}, f32[384,128]{1,0:T(8,128)S(1)}, u32[]{:S(2)}, u32[]{:S(2)}) collective-permute-start(f32[384,128]{1,0:T(8,128)S(1)} %get-tuple-element.26), channel_id=1, source_target_pairs={{0,32},{32,0},{1,33},{33,1},{2,34},{34,2},{3,35},{35,3},{4,36},{36... | collective-permute-start | bytes 589832 | tf_op jit(solution)/shard_map/ppermute | solution.py:430
  224.5 1.1 collective-permute-done
  225.6 13.6 %all_to_all.36 = f32[16,24,128]{2,1,0:T(8,128)S(1)} all-to-all(f32[16,24,128]{2,1,0:T(8,128)S(1)} %bitcast.23), channel_id=1, replica_groups=mesh['x'=4,'core'=2,'z'=8,'y'=4] {'x','y'}, dimensions={0} | all-to-all | bytes 393216 | tf_op jit(solution)/shard_map/all_to_all | solution.py:426
  239.2 10.4 %all_to_all.37 = f32[8,24,128]{2,1,0:T(8,128)S(1)} all-to-all(f32[8,24,128]{2,1,0:T(8,128)S(1)} %broadcast_in_dim.4), channel_id=1, replica_groups=mesh['x'=4,'core'=2,'z'=8,'y'=4] {'z'}, dimensions={0} | all-to-all | bytes 196608 | tf_op jit(solution)/shard_map/all_to_all | solution.py:426
  249.6 0.7 broadcast_in_dim.5.refs_5_
  250.3 3.5 %all-to-all-start.6 = ((f32[16,24,128]{2,1,0:T(8,128)}), f32[16,24,128]{2,1,0:T(8,128)S(1)}, u32[]{:S(2)}, u32[]{:S(2)}) async-start(f32[16,24,128]{2,1,0:T(8,128)} %broadcast_in_dim.5.refs_5_), calls=%async_computation.6 | async-start | bytes 393216 | tf_op jit(solution)/shard_map/all_to_all | solution.py:426
  253.9 0.0 copy-done.1
  253.9 6.9 %shard_map.153 = bf16[1,12,384,128]{3,2,1,0:T(8,128)(2,1)} custom-call(bf16[32,96,384]{2,1,0:T(8,128)(2,1)} %all-to-all-done.3.refs_1_.refs_0_, bf16[12,512,384]{2,1,0:T(8,128)(2,1)} %get-tuple-element.19.refs_1_.refs_2_, bf16[6,256,384]{2,1,0:T(8,128)(2,1)S(1)} %copy-done.2, bf16[512,128]{1,0:T(8,128)(2,1)S(1)} %copy-done.3, ...), custom_call_target="tpu_custom_call" | custom-call | flops 4000000000 | bytes 8617984 | tf_op jit(solution)/shard_map/pallas_call | solution.py:414
  260.8 0.0 all-to-all-done.6
  260.8 4.3 %collective-permute-start.1 = (f32[3,128,128]{2,1,0:T(8,128)S(1)}, f32[3,128,128]{2,1,0:T(8,128)S(1)}, u32[]{:S(2)}, u32[]{:S(2)}) collective-permute-start(f32[3,128,128]{2,1,0:T(8,128)S(1)} %bitcast.21), channel_id=1, source_target_pairs={{0,32},{32,0},{1,33},{33,1},{2,34},{34,2},{3,35},{35,3},{4,36},{36... | collective-permute-start | bytes 589832 | tf_op jit(solution)/shard_map/ppermute | solution.py:430
  265.1 1.1 collective-permute-done.1
  266.2 0.7 select_bitcast_fusion
  (9 shorter events, 0.1 us)
Async XLA Ops:
  5.6 66.1 %all-to-all-start = ((bf16[32,96,384]{2,1,0:T(8,128)(2,1)}), bf16[32,96,384]{2,1,0:T(8,128)(2,1)}, u32[]{:S(2)}, u32[]{:S(2)}) async-start(bf16[32,96,384]{2,1,0:T(8,128)(2,1)} %shard_map.144.refs_6_.refs_4_), calls=%async_computation | async-start | bytes 4718592 | tf_op jit(solution)/shard_map/all_to_all | solution.py:426
  116.9 32.7 %all-to-all-start.2 = ((bf16[32,48,384]{2,1,0:T(8,128)(2,1)}), bf16[32,48,384]{2,1,0:T(8,128)(2,1)S(1)}, u32[]{:S(2)}, u32[]{:S(2)}) async-start(bf16[32,48,384]{2,1,0:T(8,128)(2,1)} %shard_map.148.refs_1_), calls=%async_computation.2 | async-start | bytes 2359296 | tf_op jit(solution)/shard_map/all_to_all | solution.py:426
  155.3 58.2 %all-to-all-start.3 = ((bf16[32,96,384]{2,1,0:T(8,128)(2,1)}), bf16[32,96,384]{2,1,0:T(8,128)(2,1)}, u32[]{:S(2)}, u32[]{:S(2)}) async-start(bf16[32,96,384]{2,1,0:T(8,128)(2,1)} %shard_map.150.refs_6_), calls=%async_computation.3 | async-start | bytes 4718592 | tf_op jit(solution)/shard_map/all_to_all | solution.py:426
  162.4 51.2 %copy-start = (bf16[1,12,384,128]{3,2,1,0:T(8,128)(2,1)S(1)}, bf16[1,12,384,128]{3,2,1,0:T(8,128)(2,1)}, u32[]{:S(2)}) copy-start(bf16[1,12,384,128]{3,2,1,0:T(8,128)(2,1)} %param.9) | copy-start | bytes 3538948
  213.5 0.9 copy-start.4
  218.9 34.9 %copy-start.1 = (bf16[128,128]{1,0:T(8,128)(2,1)S(1)}, bf16[128,128]{1,0:T(8,128)(2,1)}, u32[]{:S(2)}) copy-start(bf16[128,128]{1,0:T(8,128)(2,1)} %refs_4_.5) | copy-start | bytes 98308
  219.0 34.9 %copy-start.2 = (bf16[6,256,384]{2,1,0:T(8,128)(2,1)S(1)}, bf16[6,256,384]{2,1,0:T(8,128)(2,1)}, u32[]{:S(2)}) copy-start(bf16[6,256,384]{2,1,0:T(8,128)(2,1)} %get-tuple-element.27.refs_2_) | copy-start | bytes 3538948
  219.0 34.9 %copy-start.3 = (bf16[512,128]{1,0:T(8,128)(2,1)S(1)}, bf16[512,128]{1,0:T(8,128)(2,1)}, u32[]{:S(2)}) copy-start(bf16[512,128]{1,0:T(8,128)(2,1)} %get-tuple-element.28.refs_3_) | copy-start | bytes 393220
  219.0 6.6 %collective-permute-start = (f32[384,128]{1,0:T(8,128)S(1)}, f32[384,128]{1,0:T(8,128)S(1)}, u32[]{:S(2)}, u32[]{:S(2)}) collective-permute-start(f32[384,128]{1,0:T(8,128)S(1)} %get-tuple-element.26), channel_id=1, source_target_pairs={{0,32},{32,0},{1,33},{33,1},{2,34},{34,2},{3,35},{35,3},{4,36},{36... | collective-permute-start | bytes 589832 | tf_op jit(solution)/shard_map/ppermute | solution.py:430
  250.3 10.5 %all-to-all-start.6 = ((f32[16,24,128]{2,1,0:T(8,128)}), f32[16,24,128]{2,1,0:T(8,128)S(1)}, u32[]{:S(2)}, u32[]{:S(2)}) async-start(f32[16,24,128]{2,1,0:T(8,128)} %broadcast_in_dim.5.refs_5_), calls=%async_computation.6 | async-start | bytes 393216 | tf_op jit(solution)/shard_map/all_to_all | solution.py:426
  260.8 5.4 %collective-permute-start.1 = (f32[3,128,128]{2,1,0:T(8,128)S(1)}, f32[3,128,128]{2,1,0:T(8,128)S(1)}, u32[]{:S(2)}, u32[]{:S(2)}) collective-permute-start(f32[3,128,128]{2,1,0:T(8,128)S(1)} %bitcast.21), channel_id=1, source_target_pairs={{0,32},{32,0},{1,33},{33,1},{2,34},{34,2},{3,35},{35,3},{4,36},{36... | collective-permute-start | bytes 589832 | tf_op jit(solution)/shard_map/ppermute | solution.py:430
